TPU v7x, 128 devices: a whole 4x4x4 slice. The times are simulated.
128 devices in a mesh: ta: 16 (over z_lo, y, core), xyz: 8 (over z_hi, x).
Axes of the slice: x: 4, y: 4, z: 4 (z_hi: 2, z_lo: 2; z = z_hi * 2 + z_lo), core: 2. Of those that a mesh axis runs over, the one named last changes fastest.
Arguments:
- fine_field: bfloat16 [16, 8, 16, 8, 2, 768], P('ta', None, 'xyz'), may hold values from -40 to 40
- null_vectors: bfloat16 [16, 8, 16, 8, 2, 32, 768], P('ta', None, 'xyz'), may hold values from -1 to 1
- coarse_links: bfloat16 [9, 32, 16, 8, 64, 128], P(None, 'ta', 'xyz'), may hold values from -0.35 to 19
Outputs:
- coarse_solution: float32 [32, 16, 8, 128], P('ta', 'xyz')
- coarse_residual: float32 [32, 16, 8, 128], P('ta', 'xyz')
All inputs are finite; a program needn't handle non-finite values.
Results may differ from a plain program's by a relative error of at most 0.004.
Values may be sent and summed in bfloat16 or wider, within the bound.
No kernel may reach another device: no remote copies, remote signals or barrier semaphores. Data moves between devices by JAX's collectives and lax.ppermute only.
A program may use at most 64 MiB of HBM per device.

v0:
```python
import jax
import jax.numpy as jnp
from jax import lax
from jax.sharding import PartitionSpec as P

TSPAN = 4
ITERS = 2


def from_behind(block, axis, distance):
    devices = range(lax.axis_size(axis))
    route = [((i - distance) % len(devices), i) for i in devices]
    return lax.ppermute(block, axis, route)


def padded_2(block, sides, width):
    for axis, dim in sides:
        count = lax.axis_size(axis)
        forward = [(i, i + 1) for i in range(count - 1)]
        forward.append((count - 1, 0))
        backward = [(target, source) for source, target in forward]
        low = lax.ppermute(
            lax.slice_in_dim(block, block.shape[dim] - width, None, axis=dim), axis, forward
        )
        high = lax.ppermute(lax.slice_in_dim(block, 0, width, axis=dim), axis, backward)
        block = jnp.concatenate([low, block, high], axis=dim)
    return block


def from_partner(block, axis, apart):
    count = lax.axis_size(axis)
    route = []
    for low in range(count):
        high = low | 1 << apart
        if high != low and high < count:
            route += [(low, high), (high, low)]
    return lax.ppermute(block, axis, route)


def rotated(values):
    pairs = values.reshape(values.shape[:-1] + (values.shape[-1] // 2, 2))
    turned = jnp.stack([pairs[..., 1], -pairs[..., 0]], axis=-1).reshape(values.shape)
    return jnp.stack([values, turned], axis=-2)


def complex_form(values):
    midpoint = values.shape[-1] // 2
    real_part = values[..., :midpoint]
    imag_part = values[..., midpoint:]
    return jnp.stack(
        [
            jnp.concatenate([real_part, -imag_part], axis=-1),
            jnp.concatenate([imag_part, real_part], axis=-1),
        ],
        axis=-2,
    )


def scaled(alpha_real, alpha_imag, values):
    midpoint = values.shape[-1] // 2
    real_part = values[..., :midpoint]
    imag_part = values[..., midpoint:]
    return jnp.concatenate(
        [
            alpha_real * real_part - alpha_imag * imag_part,
            alpha_real * imag_part + alpha_imag * real_part,
        ],
        axis=-1,
    )


def restrict_local(field, vectors):
    products = jnp.einsum(
        "xzycof,xzyckf->xzyock", rotated(field), vectors, preferred_element_type=jnp.float32
    )
    return products.reshape(products.shape[:3] + (-1,))


def apply_local(vector, coarse_links, slices):
    rounded = vector.astype(jnp.bfloat16)
    stride = slices // 2
    east = from_behind(rounded, "ta", -stride)
    west = from_behind(rounded, "ta", stride)
    padded = padded_2(rounded, (("xyz", 1),), 1)
    partner = from_partner(rounded, "ta", 0)
    later = jnp.concatenate([rounded[1:], partner[:1]], axis=0)
    earlier = jnp.concatenate([partner[1:], rounded[:1]], axis=0)
    stacked = jnp.stack(
        [
            rounded,
            east,
            west,
            jnp.roll(rounded, -1, axis=2),
            jnp.roll(rounded, 1, axis=2),
            padded[:, 2:],
            padded[:, :-2],
            later,
            earlier,
        ]
    )
    result = jnp.einsum(
        "drzyjm,drzyom->rzyoj",
        coarse_links,
        complex_form(stacked),
        preferred_element_type=jnp.float32,
    )
    return result.reshape(result.shape[:3] + (-1,))


def on_device(fine_field, null_vectors, coarse_links):
    ta_count = lax.axis_size("ta")
    slices = ta_count // TSPAN
    position = lax.axis_index("ta")
    own_slice = position // TSPAN
    partial_value = restrict_local(fine_field[0], null_vectors[0])
    marker = (jnp.arange(slices) == own_slice).astype(jnp.float32)
    spread = partial_value[:, None] * marker[None, :, None, None, None]
    merged = spread.reshape((partial_value.shape[0] * slices,) + partial_value.shape[1:])
    source = lax.psum_scatter(merged, "ta", scatter_dimension=0, tiled=True)
    solution = jnp.zeros_like(source)
    residual = source
    for iteration in range(ITERS):
        image = apply_local(residual, coarse_links, slices)
        midpoint = image.shape[-1] // 2
        image_real = image[..., :midpoint]
        image_imag = image[..., midpoint:]
        residual_real = residual[..., :midpoint]
        residual_imag = residual[..., midpoint:]
        dot_real, dot_imag, image_norm = lax.psum(
            (
                jnp.sum(image_real * residual_real + image_imag * residual_imag),
                jnp.sum(image_real * residual_imag - image_imag * residual_real),
                jnp.sum(image_real * image_real + image_imag * image_imag),
            ),
            ("ta", "xyz"),
        )
        alpha_real = dot_real / image_norm
        alpha_imag = dot_imag / image_norm
        solution = solution + scaled(alpha_real, alpha_imag, residual)
        residual = residual - scaled(alpha_real, alpha_imag, image)
    return (solution, residual)


def solution(mesh):
    in_specs = (
        P("ta", None, "xyz", None, None, None),
        P("ta", None, "xyz", None, None, None, None),
        P(None, "ta", "xyz", None, None, None),
    )
    out_specs = (P("ta", "xyz", None, None), P("ta", "xyz", None, None))
    return jax.shard_map(
        on_device, mesh=mesh, in_specs=in_specs, out_specs=out_specs, check_vma=False
    )
```

profile of v0, /device:TPU:1, one launch (start us, length us, event | category | flops | bytes accessed | tf_op | source)
XLA Modules:
  0.0 282.8 jit_solution(9100996296495934831)
XLA Ops:
  7.2 0.0 reduce-scatter.2.cloned.1.call-start
  7.2 0.1 mul.134
  7.3 6.8 %copy.98 = bf16[1,8,2,8,2,768]{3,1,5,4,2,0:T(8,128)(2,1)} copy(bf16[1,8,2,8,2,768]{5,4,3,2,1,0:T(2,128)(2,1)} %param.3) | data formatting | bytes 786432 | tf_op args[0]
  14.2 3.5 %fusion.31 = (bf16[8,2,8,2,384,1]{2,0,5,4,3,1:T(8,128)(2,1)S(1)}, bf16[8,2,8,2,384,1]{2,0,5,4,3,1:T(8,128)(2,1)S(1)}) fusion(bf16[8,2,8,2,384,2]{2,0,5,4,3,1:T(8,128)(2,1)} %bitcast.86), kind=kLoop, calls=%fused_computation.82 | loop fusion | flops 98304 | bytes 786432 | tf_op jit(solution)/shard_map/slice | solution.py:42
  17.6 4.1 %pad_maximum_fusion = bf16[8,2,8,2,384,2]{2,0,5,4,3,1:T(8,128)(2,1)} fusion(bf16[8,2,8,2,384,1]{2,0,5,4,3,1:T(8,128)(2,1)S(1)} %get-tuple-element.20, bf16[8,2,8,2,384,1]{2,0,5,4,3,1:T(8,128)(2,1)S(1)} %get-tuple-element.19), kind=kLoop, calls=%fused_computation.2 | loop fusion | flops 196608 | bytes 786432 | tf_op jit(solution)/shard_map/stack | solution.py:42
  21.7 8.9 %copy.100 = bf16[8,2,8,2,1,768]{5,4,3,2,1,0:T(2,128)(2,1)S(1)} copy(bf16[8,2,8,2,1,768]{2,0,5,3,1,4:T(8,128)(2,1)} %bitcast.87) | data formatting | bytes 786432 | tf_op jit(solution)/shard_map/stack;reshape | solution.py:43
  30.6 0.8 copy.99
  31.4 8.0 %fusion.6 = f32[8,2,8,2,2,32]{5,3,4,2,1,0:T(2,128)S(1)} fusion(bf16[1,8,2,8,2,32,768]{6,5,4,3,2,1,0:T(8,128)(2,1)} %param.4, bf16[8,2,8,2,1,768]{5,4,3,2,1,0:T(2,128)(2,1)S(1)} %copy.100, bf16[8,2,8,2,1,768]{5,4,3,2,1,0:T(2,128)(2,1)S(1)} %copy.99), kind=kOutput, calls=%fused_computation.8 | convolution fusion | flops 26738688 | bytes 13434880 | tf_op jit(solution)/shard_map/xzycof,xzyckf->xzyock/dot_general | solution.py:73
  39.3 0.1 copy.101
  39.5 0.2 mul.130
  39.7 0.8 bitcast_multiply_fusion
  40.5 0.0 reduce-scatter.2.cloned.1.call-update
  40.5 59.9 %reduce-scatter.2.cloned.1.call-done = f32[2,2,8,128]{3,2,1,0:T(8,128)} async-done(((f32[32,2,8,128]{3,2,1,0:T(8,128)}), f32[2,2,8,128]{3,2,1,0:T(8,128)}) %reduce-scatter.2.cloned.1.call-update) | async-done | bytes 16400 | tf_op jit(solution)/shard_map/reduce_scatter | solution.py:119
  100.4 0.8 constant_dynamic-update-slice_fusion.8
  101.2 4.1 %collective-permute-start = (bf16[2,2,8,128]{3,2,1,0:T(8,128)(2,1)S(1)}, bf16[2,2,8,128]{3,2,1,0:T(8,128)(2,1)S(1)}, u32[]{:S(2)}, u32[]{:S(2)}) collective-permute-start(bf16[2,2,8,128]{3,2,1,0:T(8,128)(2,1)S(1)} %get-tuple-element.18), channel_id=1, source_target_pairs={{16,0},{24,8},{32,16},{40,24},{48,32},{56,40},{64,48},{72,56},{80,... | collective-permute-start | bytes 24584 | tf_op jit(solution)/shard_map/ppermute | solution.py:13
  105.3 2.3 collective-permute-start.4
  107.6 4.9 %collective-permute-start.2 = (bf16[2,1,8,128]{3,2,1,0:T(8,128)(2,1)S(1)}, bf16[2,1,8,128]{3,2,1,0:T(8,128)(2,1)S(1)}, u32[]{:S(2)}, u32[]{:S(2)}) collective-permute-start(bf16[2,1,8,128]{3,2,1,0:T(8,128)(2,1)S(1)} %get-tuple-element.54), channel_id=1, source_target_pairs={{1,0},{2,1},{3,2},{4,3},{5,4},{6,5},{7,6},{0,7},{9,8},{10,9},{11,1... | collective-permute-start | bytes 12296 | tf_op jit(solution)/shard_map/ppermute | solution.py:25
  112.6 0.7 collective-permute-done.2
  113.3 5.3 %collective-permute-done.3 = bf16[2,1,8,128]{3,2,1,0:T(8,128)(2,1)S(1)} collective-permute-done((bf16[2,1,8,128]{3,2,1,0:T(8,128)(2,1)S(1)}, bf16[2,1,8,128]{3,2,1,0:T(8,128)(2,1)S(1)}, u32[]{:S(2)}, u32[]{:S(2)}) %collective-permute-start.3) | collective-permute-done | bytes 4128 | tf_op jit(solution)/shard_map/ppermute | solution.py:22
  118.6 0.1 slice_negate_fusion.2
  118.7 0.1 maximum_bitcast_fusion
  118.8 0.1 copy.102
  119.0 0.1 copy.103
  119.1 3.8 %fusion.9 = f32[2,2,8,2,64]{4,3,2,1,0:T(2,128)S(1)} fusion(bf16[9,2,2,8,64,128]{5,4,3,2,1,0:T(8,128)(2,1)} %param.5, bf16[9,2,2,8,1,128]{5,4,0,3,2,1:T(2,128)(2,1)S(1)} %copy.103, bf16[9,2,2,8,1,128]{5,4,0,3,2,1:T(2,128)(2,1)S(1)} %copy.102), kind=kOutput, calls=%fused_computation.9 | convolution fusion | flops 9732096 | bytes 4882432 | tf_op jit(solution)/shard_map/drzyjm,drzyom->rzyoj/dot_general | solution.py:101
  122.9 0.1 reshape.19
  123.0 0.7 add_reduce_fusion.3
  123.7 63.6 %all-reduce.1 = (f32[]{:T(128)}, f32[]{:T(128)}, f32[]{:T(128)}) all-reduce(f32[]{:T(128)} %get-tuple-element.5, f32[]{:T(128)} %get-tuple-element.7, f32[]{:T(128)} %get-tuple-element.4), channel_id=1, replica_groups=mesh['ta'=16,'xyz'=8] {'ta','xyz'}, use_global_device_ids=true, to_apply=%region_6.7 | all-reduce | flops 3 | bytes 24 | tf_op jit(solution)/shard_map/psum | solution.py:129
  189.8 0.1 multiply_subtract_fusion.2
  189.9 0.1 constant_dynamic-update-slice_fusion.17
  190.0 1.1 collective-permute-start.5
  191.1 0.3 collective-permute-start.6
  191.5 1.3 collective-permute-start.9
  192.7 0.1 multiply_subtract_fusion.3
  192.8 2.6 collective-permute-start.7
  195.5 0.2 collective-permute-done.6
  195.8 0.4 collective-permute-done.7
  196.2 5.3 %collective-permute-done.8 = bf16[2,1,8,128]{3,2,1,0:T(8,128)(2,1)S(1)} collective-permute-done((bf16[2,1,8,128]{3,2,1,0:T(8,128)(2,1)S(1)}, bf16[2,1,8,128]{3,2,1,0:T(8,128)(2,1)S(1)}, u32[]{:S(2)}, u32[]{:S(2)}) %collective-permute-start.8) | collective-permute-done | bytes 4128 | tf_op jit(solution)/shard_map/ppermute | solution.py:22
  201.6 0.1 slice_negate_fusion.1
  201.7 0.1 maximum_bitcast_fusion.2
  201.8 0.1 copy.105
  201.9 0.1 copy.106
  202.0 3.8 %fusion.12 = f32[2,2,8,2,64]{4,3,2,1,0:T(2,128)S(1)} fusion(bf16[9,2,2,8,64,128]{5,4,3,2,1,0:T(8,128)(2,1)} %param.5, bf16[9,2,2,8,1,128]{5,4,0,3,2,1:T(2,128)(2,1)S(1)} %copy.106, bf16[9,2,2,8,1,128]{5,4,0,3,2,1:T(2,128)(2,1)S(1)} %copy.105), kind=kOutput, calls=%fused_computation.10 | convolution fusion | flops 9732096 | bytes 4882432 | tf_op jit(solution)/shard_map/drzyjm,drzyom->rzyoj/dot_general | solution.py:101
  205.9 0.1 reshape.20
  206.0 0.7 add_reduce_fusion.1
  206.7 65.3 %all-reduce = (f32[]{:T(128)}, f32[]{:T(128)}, f32[]{:T(128)}) all-reduce(f32[]{:T(128)} %get-tuple-element.3, f32[]{:T(128)} %get-tuple-element.6, f32[]{:T(128)} %get-tuple-element.2), channel_id=1, replica_groups=mesh['ta'=16,'xyz'=8] {'ta','xyz'}, use_global_device_ids=true, to_apply=%region_12.13 | all-reduce | flops 3 | bytes 24 | tf_op jit(solution)/shard_map/psum | solution.py:129
  274.5 0.1 multiply_subtract_fusion
  274.6 0.7 maximum_subtract_fusion.1
  275.3 0.7 maximum_add_fusion
  (40 shorter events, 0.2 us)
Async XLA Ops:
  7.2 93.2 %reduce-scatter.2.cloned.1.call-start = ((), (), s32[]{:S(2)}) async-start(), calls=%async_computation.1 | async-start | bytes 278528 | tf_op jit(solution)/shard_map/reduce_scatter | solution.py:119
  21.7 8.9 %copy-start = (bf16[1,8,2,8,2,768]{5,4,3,2,1,0:T(2,128)(2,1)S(1)}, bf16[1,8,2,8,2,768]{5,4,3,2,1,0:T(2,128)(2,1)}, u32[]{:S(2)}) copy-start(bf16[1,8,2,8,2,768]{5,4,3,2,1,0:T(2,128)(2,1)} %param.3) | copy-start | bytes 1179652
  100.4 22.6 %copy-start.1 = (f32[2,2,8,128]{3,2,1,0:T(8,128)S(1)}, f32[2,2,8,128]{3,2,1,0:T(8,128)}, u32[]{:S(2)}) copy-start(f32[2,2,8,128]{3,2,1,0:T(8,128)} %reduce-scatter.2.cloned.1.call-done) | copy-start | bytes 49156
  101.2 11.3 %collective-permute-start = (bf16[2,2,8,128]{3,2,1,0:T(8,128)(2,1)S(1)}, bf16[2,2,8,128]{3,2,1,0:T(8,128)(2,1)S(1)}, u32[]{:S(2)}, u32[]{:S(2)}) collective-permute-start(bf16[2,2,8,128]{3,2,1,0:T(8,128)(2,1)S(1)} %get-tuple-element.18), channel_id=1, source_target_pairs={{16,0},{24,8},{32,16},{40,24},{48,32},{56,40},{64,48},{72,56},{80,... | collective-permute-start | bytes 24584 | tf_op jit(solution)/shard_map/ppermute | solution.py:13
  105.3 7.2 %collective-permute-start.1 = (bf16[2,2,8,128]{3,2,1,0:T(8,128)(2,1)S(1)}, bf16[2,2,8,128]{3,2,1,0:T(8,128)(2,1)S(1)}, u32[]{:S(2)}, u32[]{:S(2)}) collective-permute-start(bf16[2,2,8,128]{3,2,1,0:T(8,128)(2,1)S(1)} %get-tuple-element.18), channel_id=1, source_target_pairs={{112,0},{120,8},{0,16},{8,24},{16,32},{24,40},{32,48},{40,56},{48,... | collective-permute-start | bytes 24584 | tf_op jit(solution)/shard_map/ppermute | solution.py:13
  105.3 7.2 %collective-permute-start.4 = (bf16[2,2,8,128]{3,2,1,0:T(8,128)(2,1)S(1)}, bf16[2,2,8,128]{3,2,1,0:T(8,128)(2,1)S(1)}, u32[]{:S(2)}, u32[]{:S(2)}) collective-permute-start(bf16[2,2,8,128]{3,2,1,0:T(8,128)(2,1)S(1)} %get-tuple-element.18), channel_id=1, source_target_pairs={{0,8},{8,0},{16,24},{24,16},{32,40},{40,32},{48,56},{56,48},{64,72... | collective-permute-start | bytes 24584 | tf_op jit(solution)/shard_map/ppermute | solution.py:37
  107.6 5.7 %collective-permute-start.2 = (bf16[2,1,8,128]{3,2,1,0:T(8,128)(2,1)S(1)}, bf16[2,1,8,128]{3,2,1,0:T(8,128)(2,1)S(1)}, u32[]{:S(2)}, u32[]{:S(2)}) collective-permute-start(bf16[2,1,8,128]{3,2,1,0:T(8,128)(2,1)S(1)} %get-tuple-element.54), channel_id=1, source_target_pairs={{1,0},{2,1},{3,2},{4,3},{5,4},{6,5},{7,6},{0,7},{9,8},{10,9},{11,1... | collective-permute-start | bytes 12296 | tf_op jit(solution)/shard_map/ppermute | solution.py:25
  112.5 6.1 %collective-permute-start.3 = (bf16[2,1,8,128]{3,2,1,0:T(8,128)(2,1)S(1)}, bf16[2,1,8,128]{3,2,1,0:T(8,128)(2,1)S(1)}, u32[]{:S(2)}, u32[]{:S(2)}) collective-permute-start(bf16[2,1,8,128]{3,2,1,0:T(8,128)(2,1)S(1)} %get-tuple-element.53), channel_id=1, source_target_pairs={{0,1},{1,2},{2,3},{3,4},{4,5},{5,6},{6,7},{7,0},{8,9},{9,10},{10,1... | collective-permute-start | bytes 12296 | tf_op jit(solution)/shard_map/ppermute | solution.py:22
  190.0 5.5 %collective-permute-start.5 = (bf16[2,2,8,128]{3,2,1,0:T(8,128)(2,1)S(1)}, bf16[2,2,8,128]{3,2,1,0:T(8,128)(2,1)S(1)}, u32[]{:S(2)}, u32[]{:S(2)}) collective-permute-start(bf16[2,2,8,128]{3,2,1,0:T(8,128)(2,1)S(1)} %get-tuple-element.15), channel_id=1, source_target_pairs={{16,0},{24,8},{32,16},{40,24},{48,32},{56,40},{64,48},{72,56},{80,... | collective-permute-start | bytes 24584 | tf_op jit(solution)/shard_map/ppermute | solution.py:13
  191.1 4.6 %collective-permute-start.6 = (bf16[2,2,8,128]{3,2,1,0:T(8,128)(2,1)S(1)}, bf16[2,2,8,128]{3,2,1,0:T(8,128)(2,1)S(1)}, u32[]{:S(2)}, u32[]{:S(2)}) collective-permute-start(bf16[2,2,8,128]{3,2,1,0:T(8,128)(2,1)S(1)} %get-tuple-element.15), channel_id=1, source_target_pairs={{112,0},{120,8},{0,16},{8,24},{16,32},{24,40},{32,48},{40,56},{48,... | collective-permute-start | bytes 24584 | tf_op jit(solution)/shard_map/ppermute | solution.py:13
  191.5 4.3 %collective-permute-start.9 = (bf16[2,2,8,128]{3,2,1,0:T(8,128)(2,1)S(1)}, bf16[2,2,8,128]{3,2,1,0:T(8,128)(2,1)S(1)}, u32[]{:S(2)}, u32[]{:S(2)}) collective-permute-start(bf16[2,2,8,128]{3,2,1,0:T(8,128)(2,1)S(1)} %get-tuple-element.15), channel_id=1, source_target_pairs={{0,8},{8,0},{16,24},{24,16},{32,40},{40,32},{48,56},{56,48},{64,72... | collective-permute-start | bytes 24584 | tf_op jit(solution)/shard_map/ppermute | solution.py:37
  192.8 3.4 %collective-permute-start.7 = (bf16[2,1,8,128]{3,2,1,0:T(8,128)(2,1)S(1)}, bf16[2,1,8,128]{3,2,1,0:T(8,128)(2,1)S(1)}, u32[]{:S(2)}, u32[]{:S(2)}) collective-permute-start(bf16[2,1,8,128]{3,2,1,0:T(8,128)(2,1)S(1)} %get-tuple-element.44), channel_id=1, source_target_pairs={{1,0},{2,1},{3,2},{4,3},{5,4},{6,5},{7,6},{0,7},{9,8},{10,9},{11,1... | collective-permute-start | bytes 12296 | tf_op jit(solution)/shard_map/ppermute | solution.py:25
  195.5 6.1 %collective-permute-start.8 = (bf16[2,1,8,128]{3,2,1,0:T(8,128)(2,1)S(1)}, bf16[2,1,8,128]{3,2,1,0:T(8,128)(2,1)S(1)}, u32[]{:S(2)}, u32[]{:S(2)}) collective-permute-start(bf16[2,1,8,128]{3,2,1,0:T(8,128)(2,1)S(1)} %get-tuple-element.43), channel_id=1, source_target_pairs={{0,1},{1,2},{2,3},{3,4},{4,5},{5,6},{6,7},{7,0},{8,9},{9,10},{10,1... | collective-permute-start | bytes 12296 | tf_op jit(solution)/shard_map/ppermute | solution.py:22
Sparse Core Ops, SparseCore 0:
  40.7 59.6 reduce-scatter.1
where the time goes:
time: 284 us; the launch traced here: 283 us
  blocking collectives  129 us (45%)
  waiting for transfers between devices  71.8 us (25%)
  between operations  19.2 us (7%)
  local copies, waits for them, and re-layouts  17.7 us (6%)
  starting transfers between devices  16.7 us (6%)
  matrix products  15.6 us (5%)
  other arithmetic  12.8 us (5%)
    psum x2, blocking collectives, on_device(): lax.psum((jnp.sum(image_real * residual_real + image_imag * residual_imag...  129 us
    reduce_scatter x1, waiting for transfers between devices, on_device(): source = lax.psum_scatter(merged, 'ta', scatter_dimension=0, tiled=True)  59.9 us
    ppermute x2, waiting for transfers between devices, padded_2(): lax.ppermute(lax.slice_in_dim(block, block.shape[dim] - width, None, axis...  10.6 us
    another operation x2, local copies, waits for them, and re-layouts, rotated(): return jnp.stack([values, turned], axis=-2)  9.66 us
    dot_general x1, matrix products, restrict_local(): jnp.einsum('xzycof,xzyckf->xzyock', rotated(field), vectors, preferred_el...  7.96 us
    dot_general x2, matrix products, apply_local(): jnp.einsum('drzyjm,drzyom->rzyoj', coarse_links, complex_form(stacked), p...  7.69 us
    ppermute x2, starting transfers between devices, padded_2(): lax.ppermute(lax.slice_in_dim(block, 0, width, axis=dim), axis, backward)  7.55 us
    unnamed x9, local copies, waits for them, and re-layouts  6.87 us
  transfers between devices with their start and end apart: 11, of which 6 were waited for; matrix products, arithmetic and copies ran while one was open for 0% of the time, Pallas kernels for 0%

commit v1 on v0

v1 whole, which is shorter than its diff:
```python
import jax
import jax.numpy as jnp
from jax import lax
from jax.experimental import pallas as pl
from jax.experimental.pallas import tpu as pltpu
from jax.sharding import PartitionSpec as P

TSPAN = 4
HALF = 64
WIDE = 128
BF16 = jnp.bfloat16
F32 = jnp.float32
VMEM = pl.BlockSpec(memory_space=pltpu.VMEM)
LIMIT = 40 * 1024 * 1024


def iota(shape, dim):
    return lax.broadcasted_iota(jnp.int32, shape, dim)


def halves_swapped(values):
    return pltpu.roll(values, HALF, values.ndim - 1)


def own_site(products):
    folded = []
    row, lane = iota((8, WIDE), 0), iota((8, WIDE), 1)
    for o in range(2):
        total = jnp.zeros((8, WIDE), F32)
        for pair in range(4):
            block = products[o * 8 : o * 8 + 8, pair * WIDE : (pair + 1) * WIDE]
            total = total + jnp.where(row == 2 * pair + lane // HALF, block, 0.0)
        folded.append(total + halves_swapped(total))
    return jnp.where(lane < HALF, folded[0], folded[1])


def restrict_kernel(field_ref, vectors_ref, send_ref):
    x = pl.program_id(0)
    count = pl.num_programs(0)
    half = lax.axis_index("ta") // 8
    even = iota((16, 768), 1) % 2 == 0
    parts = []
    for z in range(2):
        values = field_ref[0, 0, z].astype(F32)
        values = jnp.concatenate([values[:, 0, :], values[:, 1, :]], axis=0)
        after = pltpu.roll(values, 767, 1)
        before = pltpu.roll(values, 1, 1)
        turned = jnp.where(even, after, -before)
        rows = jnp.concatenate([values, turned], axis=0).astype(BF16)
        vectors = vectors_ref[0, 0, z].reshape(512, 768)
        products = lax.dot_general(
            rows, vectors, (((1,), (1,)), ((), ())), preferred_element_type=F32
        )
        first = iota((8, 512), 1) // 32 % 2 == 0
        products = jnp.concatenate(
            [
                jnp.where(first, products[o * 16 : o * 16 + 8], products[o * 16 + 8 : o * 16 + 16])
                for o in range(2)
            ],
            axis=0,
        )
        parts.append(own_site(products))
    partial = jnp.stack(parts)
    high = partial.astype(BF16)
    low = (partial - high.astype(F32)).astype(BF16)
    behind = lax.rem(x + count - 1, count)
    ahead = lax.rem(x + 1, count)
    send_ref[2 * x + half, 0] = high
    send_ref[2 * x + half, 1] = low
    send_ref[2 * x + 1 - half, 0] = high
    send_ref[2 * x + 1 - half, 1] = low
    send_ref[2 * behind + half, 2] = high
    send_ref[2 * ahead + half, 3] = high
    send_ref[2 * x + 1 - half, 2] = high
    send_ref[2 * x + 1 - half, 3] = high


def gather_kernel(received_ref, source_ref, own_ref, other_ref, plus_ref, minus_ref):
    half = lax.axis_index("ta") % 2

    def summed(first, slots):
        rows = []
        for s in range(2):
            total = None
            for i in range(TSPAN):
                for slot in slots:
                    term = received_ref[first + s * TSPAN + i, slot].astype(F32)
                    total = term if total is None else total + term
            rows.append(total)
        return jnp.stack(rows)

    source = summed(8 * half, (0, 1))
    source_ref[...] = source
    own_ref[...] = source.astype(BF16)
    other_ref[...] = summed(8 - 8 * half, (0, 1)).astype(BF16)
    plus_ref[...] = summed(8 * half, (2,)).astype(BF16)
    minus_ref[...] = summed(8 * half, (3,)).astype(BF16)


def forms(v):
    lane = iota((8, WIDE), 1)
    return jnp.concatenate([jnp.where(lane < HALF, v, -v), halves_swapped(v)], axis=0).astype(BF16)


def applied(links_ref, own, other, plus, minus, up, down):
    rounded = own.astype(BF16).astype(F32)
    low = own - rounded
    plain, full = [], []
    for r in range(2):
        for z in range(2):
            here = rounded[r, z]
            neighbours = [
                here,
                plus[r, z],
                minus[r, z],
                pltpu.roll(here, 7, 0),
                pltpu.roll(here, 1, 0),
                rounded[r, 1] if z == 0 else up[r],
                down[r] if z == 0 else rounded[r, 0],
                rounded[1, z] if r == 0 else other[0, z],
                other[1, z] if r == 0 else rounded[0, z],
            ]
            matrices = [links_ref[d, r, z].reshape(512, WIDE) for d in range(9)]
            rows = [forms(v) for v in neighbours]
            total = lax.dot_general(
                jnp.concatenate([rows[0], forms(low[r, z])], axis=0),
                matrices[0],
                (((1,), (1,)), ((), ())),
                preferred_element_type=F32,
            )
            main = total[:16]
            for d in range(1, 9, 2):
                main = main + lax.dot_general(
                    jnp.concatenate(rows[d : d + 2], axis=1),
                    jnp.concatenate(matrices[d : d + 2], axis=1),
                    (((1,), (1,)), ((), ())),
                    preferred_element_type=F32,
                )
            value = own_site(main)
            plain.append(value)
            full.append(value + own_site(total[16:]))
    shape = (2, 2, 8, WIDE)
    return jnp.stack(plain).reshape(shape), jnp.stack(full).reshape(shape)


def first_kernel(links_ref, source_ref, other_ref, plus_ref, minus_ref, up_ref, down_ref, image_ref, full_ref, own_ref):
    image, full = applied(
        links_ref,
        source_ref[...],
        other_ref[...].astype(F32),
        plus_ref[...].astype(F32),
        minus_ref[...].astype(F32),
        up_ref[...].astype(F32),
        down_ref[...].astype(F32),
    )
    image_ref[...] = image
    full_ref[...] = full
    own_ref[...] = image.astype(BF16)


def turned_back(values):
    lane = iota(values.shape, values.ndim - 1)
    swapped = halves_swapped(values)
    return jnp.where(lane < HALF, swapped, -swapped)


def second_kernel(
    links_ref, source_ref, image_ref, full_ref, other_ref, plus_ref, minus_ref, up_ref, down_ref, twice_ref, sums_ref
):
    image = image_ref[...]
    _, twice = applied(
        links_ref,
        image,
        other_ref[...].astype(F32),
        plus_ref[...].astype(F32),
        minus_ref[...].astype(F32),
        up_ref[...].astype(F32),
        down_ref[...].astype(F32),
    )
    twice_ref[...] = twice
    source = source_ref[...]
    full = full_ref[...]
    rows = []

    def add(a, b):
        rows.append(jnp.sum((a * b).reshape(32, WIDE), axis=0, keepdims=True))

    def add_complex(a, b):
        add(a, b)
        add(a, turned_back(b))

    add_complex(image, source)
    add_complex(full, source)
    add_complex(full, image)
    add_complex(twice, source)
    add_complex(twice, image)
    add_complex(full, twice)
    add(image, image)
    add(full, full)
    add(twice, twice)
    rows.append(jnp.zeros((1, WIDE), F32))
    sums = jnp.sum(jnp.concatenate(rows, axis=0), axis=1, keepdims=True)
    line = jnp.sum(
        jnp.where(iota((16, WIDE), 0) == iota((16, WIDE), 1), sums, 0.0), axis=0, keepdims=True
    )
    sums_ref[...] = jnp.broadcast_to(line.reshape(1, 1, WIDE), sums_ref.shape)


def last_kernel(sums_ref, source_ref, image_ref, full_ref, twice_ref, solution_ref, residual_ref):
    line = jnp.sum(sums_ref[...], axis=0)

    def at(k):
        return line[:, k : k + 1]

    def times(a, b):
        return a[0] * b[0] - a[1] * b[1], a[0] * b[1] + a[1] * b[0]

    def pair(k):
        return at(2 * k), at(2 * k + 1)

    image_source, full_source, full_image, twice_source, twice_image, full_twice = (pair(k) for k in range(6))
    image_norm, full_norm, twice_norm = at(12), at(13), at(14)
    alpha = image_source[0] / image_norm, image_source[1] / image_norm
    conj = alpha[0], -alpha[1]
    size = alpha[0] * alpha[0] + alpha[1] * alpha[1]
    term_a = times(alpha, full_image)
    term_b = times(conj, twice_source)
    dot = (
        full_source[0] - term_a[0] - term_b[0] + size * twice_image[0],
        full_source[1] - term_a[1] - term_b[1] + size * twice_image[1],
    )
    norm = full_norm - 2.0 * times(alpha, full_twice)[0] + size * twice_norm
    beta = dot[0] / norm, dot[1] / norm

    def scaled(a, values):
        return a[0] * values - a[1] * turned_back(values)

    source = source_ref[...]
    residual = source - scaled(alpha, image_ref[...])
    second = full_ref[...] - scaled(alpha, twice_ref[...])
    solution_ref[...] = scaled(alpha, source) + scaled(beta, residual)
    residual_ref[...] = residual - scaled(beta, second)


def shift(block, axis, distance):
    count = lax.axis_size(axis)
    return lax.ppermute(block, axis, [(i, (i + distance) % count) for i in range(count)])


def from_core(block):
    return lax.ppermute(block, "ta", [(i, i ^ 1) for i in range(lax.axis_size("ta"))])


def struct(shape, dtype=F32):
    return jax.ShapeDtypeStruct(shape, dtype)


def params():
    return pltpu.CompilerParams(vmem_limit_bytes=LIMIT)


def halo(own):
    count_ta, count_xyz = lax.axis_size("ta"), lax.axis_size("xyz")
    other = from_core(own)
    odd = lax.axis_index("ta") % 2 == 1
    chip = jnp.concatenate([own, other], axis=0)
    along_x = lax.ppermute(
        chip, "ta", [(i, (i + (2 if i % 2 == 0 else -2)) % count_ta) for i in range(count_ta)]
    )
    along_z = lax.ppermute(
        jnp.where(odd, chip[:, 0], chip[:, 1]),
        ("ta", "xyz"),
        [
            (i * count_xyz + j, i * count_xyz + (j + (1 if i % 2 == 0 else -1)) % count_xyz)
            for i in range(count_ta)
            for j in range(count_xyz)
        ],
    )
    back = jnp.concatenate([along_x[2:], along_z[2:, None]], axis=1)
    swapped = from_core(back)
    mine = jnp.concatenate([along_x[:2], along_z[:2, None]], axis=1)
    plus = jnp.where(odd, mine, swapped)
    minus = jnp.where(odd, swapped, mine)
    return other, plus[:, :2], minus[:, :2], plus[:, 2], minus[:, 2]


def on_device(fine_field, null_vectors, coarse_links):
    field4 = (2, 2, 8, WIDE)
    send = pl.pallas_call(
        restrict_kernel,
        grid=(8,),
        in_specs=[
            pl.BlockSpec((1, 1, 2, 8, 2, 768), lambda x: (0, x, 0, 0, 0, 0)),
            pl.BlockSpec((1, 1, 2, 8, 2, 32, 768), lambda x: (0, x, 0, 0, 0, 0, 0)),
        ],
        out_specs=pl.BlockSpec((16, 4, 2, 8, WIDE), lambda x: (0, 0, 0, 0, 0)),
        out_shape=struct((16, 4, 2, 8, WIDE), BF16),
        compiler_params=params(),
        name="restrict",
    )(fine_field, null_vectors)
    received = lax.all_to_all(send, "ta", 0, 0)
    source, own, other, plus, minus = pl.pallas_call(
        gather_kernel,
        in_specs=[VMEM],
        out_specs=[VMEM] * 5,
        out_shape=[struct(field4)] + [struct(field4, BF16)] * 4,
        compiler_params=params(),
        name="gather",
    )(received)
    down = shift(own[:, 1], "xyz", 1)
    up = shift(own[:, 0], "xyz", -1)
    image, full, own = pl.pallas_call(
        first_kernel,
        in_specs=[VMEM] * 7,
        out_specs=[VMEM] * 3,
        out_shape=[struct(field4), struct(field4), struct(field4, BF16)],
        compiler_params=params(),
        name="first",
    )(coarse_links, source, other, plus, minus, up, down)
    twice, sums = pl.pallas_call(
        second_kernel,
        in_specs=[VMEM] * 9,
        out_specs=[VMEM] * 2,
        out_shape=[struct(field4), struct((128, 1, WIDE))],
        compiler_params=params(),
        name="second",
    )(coarse_links, source, image, full, *halo(own))
    sums = lax.all_to_all(sums, ("ta", "xyz"), 0, 0)
    return pl.pallas_call(
        last_kernel,
        in_specs=[VMEM] * 5,
        out_specs=[VMEM] * 2,
        out_shape=[struct(field4)] * 2,
        compiler_params=params(),
        name="last",
    )(sums, source, image, full, twice)


def solution(mesh):
    in_specs = (
        P("ta", None, "xyz", None, None, None),
        P("ta", None, "xyz", None, None, None, None),
        P(None, "ta", "xyz", None, None, None),
    )
    out_specs = (P("ta", "xyz", None, None), P("ta", "xyz", None, None))
    return jax.shard_map(
        on_device, mesh=mesh, in_specs=in_specs, out_specs=out_specs, check_vma=False
    )
```

time: 284 us -> 70.5 us (0.25)
  blocking collectives: 129 us -> 28.8 us
  waiting for transfers between devices: 71.8 us -> 10.2 us
  between operations: 19.2 us -> 0.72 us
  matrix products: 15.6 us -> 0 us
  other arithmetic: 12.8 us -> 0.02 us
  local copies, waits for them, and re-layouts: 17.7 us -> 7.95 us
  Pallas kernels: 0 us -> 9.41 us
  starting transfers between devices: 16.7 us -> 13.2 us
    psum x2 -> x0, blocking collectives: 129 us -> none  [on_device(): lax.psum((jnp.sum(image_real * residual_real + image_imag * residual_imag...]
    reduce_scatter x1 -> x0, waiting for transfers between devices: 59.9 us -> none  [on_device(): source = lax.psum_scatter(merged, 'ta', scatter_dimension=0, tiled=True)]
    all_to_all x0 -> x2, blocking collectives: none -> 28.8 us  [the longest x1 14.5 us: on_device(): sums = lax.all_to_all(sums, ('ta', 'xyz'), 0, 0)]
    dot_general x3 -> x0, matrix products: 15.6 us -> none  [the longest x1 7.96 us: restrict_local(): jnp.einsum('xzycof,xzyckf->xzyock', rotated(field), vectors, preferred_el...]
    another operation x6 -> x0, local copies, waits for them, and re-layouts: 10.1 us -> none  [the longest x2 9.66 us: rotated(): return jnp.stack([values, turned], axis=-2)]
    pallas_call x0 -> x5, Pallas kernels: none -> 9.41 us  [the longest x1 5.11 us: on_device(): pl.pallas_call(restrict_kernel, grid=(8,), in_specs=[pl.BlockSpec((1, 1,...]
    another operation x5 -> x0, other arithmetic: 4.32 us -> none  [the longest x1 4.07 us: rotated(): jnp.stack([pairs[..., 1], -pairs[..., 0]], axis=-1).reshape(values.shape)]
    ppermute x10 -> x6, starting transfers between devices: 16.7 us -> 13.2 us  [the longest x2 7.39 us: from_core(): lax.ppermute(block, 'ta', [(i, i ^ 1) for i in range(lax.axis_size('ta'))])]
  transfers between devices with their start and end apart: 11 -> 6, of which waited for: 6 -> 6; matrix products, arithmetic and copies ran while one was open for 0% -> 0% of each run, Pallas kernels for 0% -> 0%
where the time goes in v1:
time: 70.5 us; the launch traced here: 70.3 us
  blocking collectives  28.8 us (41%)
  starting transfers between devices  13.2 us (19%)
  waiting for transfers between devices  10.2 us (14%)
  Pallas kernels  9.41 us (13%)
  local copies, waits for them, and re-layouts  7.95 us (11%)
  between operations  0.72 us (1%)
    all_to_all x1, blocking collectives, on_device(): sums = lax.all_to_all(sums, ('ta', 'xyz'), 0, 0)  14.5 us
    all_to_all x1, blocking collectives, on_device(): received = lax.all_to_all(send, 'ta', 0, 0)  14.3 us
    unnamed x9, local copies, waits for them, and re-layouts  7.92 us
    ppermute x2, starting transfers between devices, from_core(): lax.ppermute(block, 'ta', [(i, i ^ 1) for i in range(lax.axis_size('ta'))])  7.39 us
    ppermute x2, waiting for transfers between devices, shift(): lax.ppermute(block, axis, [(i, (i + distance) % count) for i in range(cou...  6.07 us
    ppermute x2, starting transfers between devices, shift(): lax.ppermute(block, axis, [(i, (i + distance) % count) for i in range(cou...  5.57 us
    pallas_call x1, Pallas kernels, on_device(): pl.pallas_call(restrict_kernel, grid=(8,), in_specs=[pl.BlockSpec((1, 1,...  5.11 us
    ppermute x1, waiting for transfers between devices, halo(): lax.ppermute(jnp.where(odd, chip[:, 0], chip[:, 1]), ('ta', 'xyz'), [(i *...  2.28 us
  transfers between devices with their start and end apart: 6, of which 6 were waited for; matrix products, arithmetic and copies ran while one was open for 0% of the time, Pallas kernels for 0%

profile of v1, /device:TPU:1, one launch (start us, length us, event | category | flops | bytes accessed | tf_op | source)
XLA Modules:
  0.0 70.3 jit_solution(4339987795660878357)
XLA Ops:
  0.6 0.0 copy-start.2
  0.6 4.6 %copy-done.2 = bf16[1,8,2,8,2,32,768]{6,5,4,3,2,1,0:T(8,128)(2,1)S(1)} copy-done((bf16[1,8,2,8,2,32,768]{6,5,4,3,2,1,0:T(8,128)(2,1)S(1)}, bf16[1,8,2,8,2,32,768]{6,5,4,3,2,1,0:T(8,128)(2,1)}, u32[]{:S(2)}) %copy-start.2) | copy-done | bytes 12582936
  5.2 0.0 copy-start.3
  5.2 1.0 %copy-done.3 = bf16[1,8,2,8,2,768]{5,4,3,2,1,0:T(2,128)(2,1)S(1)} copy-done((bf16[1,8,2,8,2,768]{5,4,3,2,1,0:T(2,128)(2,1)S(1)}, bf16[1,8,2,8,2,768]{5,4,3,2,1,0:T(2,128)(2,1)}, u32[]{:S(2)}) %copy-start.3) | copy-done | bytes 393240
  6.2 0.0 copy-start
  6.2 5.1 %restrict.1 = bf16[16,4,2,8,128]{4,3,2,1,0:T(8,128)(2,1)S(1)} custom-call(bf16[1,8,2,8,2,768]{5,4,3,2,1,0:T(2,128)(2,1)S(1)} %copy-done.3, bf16[1,8,2,8,2,32,768]{6,5,4,3,2,1,0:T(8,128)(2,1)S(1)} %copy-done.2), custom_call_target="tpu_custom_call" | custom-call | tf_op jit(solution)/shard_map/restrict/pallas_call | solution.py:289
  11.3 14.3 %all_to_all.10.received_ref = bf16[16,4,2,8,128]{4,3,2,1,0:T(8,128)(2,1)S(1)} all-to-all(bf16[16,4,2,8,128]{4,3,2,1,0:T(8,128)(2,1)S(1)} %restrict.1), channel_id=1, replica_groups=mesh['ta'=16,'xyz'=8] {'ta'}, dimensions={0} | all-to-all | bytes 524288 | tf_op jit(solution)/shard_map/all_to_all | solution.py:301
  25.7 5.6 %collective-permute-start = (bf16[2,8,128]{2,1,0:T(8,128)(2,1)S(1)}, bf16[2,8,128]{2,1,0:T(8,128)(2,1)S(1)}, u32[]{:S(2)}, u32[]{:S(2)}) collective-permute-start(bf16[2,8,128]{2,1,0:T(8,128)(2,1)S(1)} %get-tuple-element.31), channel_id=1, source_target_pairs={{0,7},{1,0},{2,1},{3,2},{4,3},{5,4},{6,5},{7,6},{8,15},{9,8},{10,9... | collective-permute-start | bytes 12296 | tf_op jit(solution)/shard_map/ppermute | solution.py:247
  31.2 0.0 collective-permute-start.1
  31.2 0.8 %collective-permute-done.up_ref = bf16[2,8,128]{2,1,0:T(8,128)(2,1)S(1)} collective-permute-done((bf16[2,8,128]{2,1,0:T(8,128)(2,1)S(1)}, bf16[2,8,128]{2,1,0:T(8,128)(2,1)S(1)}, u32[]{:S(2)}, u32[]{:S(2)}) %collective-permute-start) | collective-permute-done | bytes 4128 | tf_op jit(solution)/shard_map/ppermute | solution.py:247
  32.0 5.3 %collective-permute-done.1.down_ref = bf16[2,8,128]{2,1,0:T(8,128)(2,1)S(1)} collective-permute-done((bf16[2,8,128]{2,1,0:T(8,128)(2,1)S(1)}, bf16[2,8,128]{2,1,0:T(8,128)(2,1)S(1)}, u32[]{:S(2)}, u32[]{:S(2)}) %collective-permute-start.1) | collective-permute-done | bytes 4128 | tf_op jit(solution)/shard_map/ppermute | solution.py:247
  37.3 0.0 copy-done
  37.3 1.5 %first.1 = (f32[2,2,8,128]{3,2,1,0:T(8,128)S(1)}, f32[2,2,8,128]{3,2,1,0:T(8,128)S(1)}, bf16[2,2,8,128]{3,2,1,0:T(8,128)(2,1)S(1)}) custom-call(bf16[9,2,2,8,64,128]{5,4,3,2,1,0:T(8,128)(2,1)S(1)} %copy-done, f32[2,2,8,128]{3,2,1,0:T(8,128)S(1)} %get-tuple-element.12.source_ref, bf16[2,2,8,128]{3,2,1,0:T(8,128)(2,1)S(1)} %get-tuple-element.13.other_ref, ...), custom_call_target="tpu_custom_call" | custom-call | tf_op jit(solution)/shard_map/first/pallas_call | solution.py:312
  38.8 2.3 %collective-permute-start.2 = (bf16[2,2,8,128]{3,2,0,1:T(8,128)(2,1)S(1)}, bf16[2,2,8,128]{3,2,0,1:T(8,128)(2,1)S(1)}, u32[]{:S(2)}, u32[]{:S(2)}) collective-permute-start(bf16[2,2,8,128]{3,2,0,1:T(8,128)(2,1)S(1)} %get-tuple-element.29), channel_id=1, source_target_pairs={{0,8},{8,0},{16,24},{24,16},{32,40},{40,32},{48,56},{56,48},{64,72... | collective-permute-start | bytes 24584 | tf_op jit(solution)/shard_map/ppermute | solution.py:251
  41.1 0.8 %collective-permute-done.2 = bf16[2,2,8,128]{3,2,0,1:T(8,128)(2,1)S(1)} collective-permute-done((bf16[2,2,8,128]{3,2,0,1:T(8,128)(2,1)S(1)}, bf16[2,2,8,128]{3,2,0,1:T(8,128)(2,1)S(1)}, u32[]{:S(2)}, u32[]{:S(2)}) %collective-permute-start.2) | collective-permute-done | bytes 8224 | tf_op jit(solution)/shard_map/ppermute | solution.py:251
  42.0 0.0 collective-permute-start.4
  42.0 0.2 collective-permute-start.3
  42.2 2.3 %collective-permute-done.4 = bf16[4,8,128]{2,1,0:T(8,128)(2,1)S(1)} collective-permute-done((bf16[4,8,128]{2,1,0:T(8,128)(2,1)S(1)}, bf16[4,8,128]{2,1,0:T(8,128)(2,1)S(1)}, u32[]{:S(2)}, u32[]{:S(2)}) %collective-permute-start.4) | collective-permute-done | bytes 8224 | tf_op jit(solution)/shard_map/ppermute | solution.py:270
  44.5 0.2 collective-permute-done.3
  44.7 5.1 %collective-permute-start.5 = (bf16[2,3,8,128]{3,2,0,1:T(8,128)(2,1)S(1)}, bf16[2,3,8,128]{3,2,0,1:T(8,128)(2,1)S(1)}, u32[]{:S(2)}, u32[]{:S(2)}) collective-permute-start(bf16[2,3,8,128]{3,2,0,1:T(8,128)(2,1)S(1)} %pad_maximum_fusion.1), channel_id=1, source_target_pairs={{0,8},{8,0},{16,24},{24,16},{32,40},{40,32},{48,56},{56,48},{64,72... | collective-permute-start | bytes 36872 | tf_op jit(solution)/shard_map/ppermute | solution.py:251
  49.7 0.8 %collective-permute-done.5 = bf16[2,3,8,128]{3,2,0,1:T(8,128)(2,1)S(1)} collective-permute-done((bf16[2,3,8,128]{3,2,0,1:T(8,128)(2,1)S(1)}, bf16[2,3,8,128]{3,2,0,1:T(8,128)(2,1)S(1)}, u32[]{:S(2)}, u32[]{:S(2)}) %collective-permute-start.5) | collective-permute-done | bytes 12320 | tf_op jit(solution)/shard_map/ppermute | solution.py:251
  50.6 0.0 copy-start.1
  50.6 2.3 %copy-done.1 = bf16[9,2,2,8,64,128]{5,4,3,2,1,0:T(8,128)(2,1)S(1)} copy-done((bf16[9,2,2,8,64,128]{5,4,3,2,1,0:T(8,128)(2,1)S(1)}, bf16[9,2,2,8,64,128]{5,4,3,2,1,0:T(8,128)(2,1)}, u32[]{:S(2)}) %copy-start.1) | copy-done | bytes 4718616
  53.0 1.7 %second.1 = (f32[2,2,8,128]{3,2,1,0:T(8,128)S(1)}, f32[128,1,128]{2,1,0:T(1,128)S(1)}) custom-call(bf16[9,2,2,8,64,128]{5,4,3,2,1,0:T(8,128)(2,1)S(1)} %copy-done.1, f32[2,2,8,128]{3,2,1,0:T(8,128)S(1)} %get-tuple-element.12.source_ref, f32[2,2,8,128]{3,2,1,0:T(8,128)S(1)} %get-tuple-element.17.image_ref, f32[2,2,8,128]{3,2,1,0:T(8,128)S(1)} %get-tuple-element.18.full_ref, ...), custom_call_target="tpu_custom_call" | custom-call | tf_op jit(solution)/shard_map/second/pallas_call | solution.py:320
  54.6 14.5 %all_to_all.11.sums_ref = f32[128,1,128]{2,1,0:T(1,128)S(1)} all-to-all(f32[128,1,128]{2,1,0:T(1,128)S(1)} %get-tuple-element.20), channel_id=1, replica_groups=mesh['ta'=16,'xyz'=8] {'ta','xyz'}, dimensions={0} | all-to-all | bytes 131072 | tf_op jit(solution)/shard_map/all_to_all | solution.py:328
  69.1 1.1 %last.1 = (f32[2,2,8,128]{3,2,1,0:T(8,128)}, f32[2,2,8,128]{3,2,1,0:T(8,128)}) custom-call(f32[128,1,128]{2,1,0:T(1,128)S(1)} %all_to_all.11.sums_ref, f32[2,2,8,128]{3,2,1,0:T(8,128)S(1)} %get-tuple-element.12.source_ref, f32[2,2,8,128]{3,2,1,0:T(8,128)S(1)} %get-tuple-element.17.image_ref, f32[2,2,8,128]{3,2,1,0:T(8,128)S(1)} %get-tuple-element.18.full_ref, ...), custom_call_target="tpu_custom_call" | custom-call | tf_op jit(solution)/shard_map/last/pallas_call | solution.py:329
  (15 shorter events, 0.1 us)
Async XLA Ops:
  0.6 4.6 %copy-start.2 = (bf16[1,8,2,8,2,32,768]{6,5,4,3,2,1,0:T(8,128)(2,1)S(1)}, bf16[1,8,2,8,2,32,768]{6,5,4,3,2,1,0:T(8,128)(2,1)}, u32[]{:S(2)}) copy-start(bf16[1,8,2,8,2,32,768]{6,5,4,3,2,1,0:T(8,128)(2,1)} %vectors_ref.1) | copy-start | bytes 37748740
  5.2 1.0 %copy-start.3 = (bf16[1,8,2,8,2,768]{5,4,3,2,1,0:T(2,128)(2,1)S(1)}, bf16[1,8,2,8,2,768]{5,4,3,2,1,0:T(2,128)(2,1)}, u32[]{:S(2)}) copy-start(bf16[1,8,2,8,2,768]{5,4,3,2,1,0:T(2,128)(2,1)} %field_ref.1) | copy-start | bytes 1179652
  6.2 31.1 %copy-start = (bf16[9,2,2,8,64,128]{5,4,3,2,1,0:T(8,128)(2,1)S(1)}, bf16[9,2,2,8,64,128]{5,4,3,2,1,0:T(8,128)(2,1)}, u32[]{:S(2)}) copy-start(bf16[9,2,2,8,64,128]{5,4,3,2,1,0:T(8,128)(2,1)} %links_ref.3) | copy-start | bytes 14155780
  25.7 6.3 %collective-permute-start = (bf16[2,8,128]{2,1,0:T(8,128)(2,1)S(1)}, bf16[2,8,128]{2,1,0:T(8,128)(2,1)S(1)}, u32[]{:S(2)}, u32[]{:S(2)}) collective-permute-start(bf16[2,8,128]{2,1,0:T(8,128)(2,1)S(1)} %get-tuple-element.31), channel_id=1, source_target_pairs={{0,7},{1,0},{2,1},{3,2},{4,3},{5,4},{6,5},{7,6},{8,15},{9,8},{10,9... | collective-permute-start | bytes 12296 | tf_op jit(solution)/shard_map/ppermute | solution.py:247
  31.2 6.1 %collective-permute-start.1 = (bf16[2,8,128]{2,1,0:T(8,128)(2,1)S(1)}, bf16[2,8,128]{2,1,0:T(8,128)(2,1)S(1)}, u32[]{:S(2)}, u32[]{:S(2)}) collective-permute-start(bf16[2,8,128]{2,1,0:T(8,128)(2,1)S(1)} %get-tuple-element.30), channel_id=1, source_target_pairs={{0,1},{1,2},{2,3},{3,4},{4,5},{5,6},{6,7},{7,0},{8,9},{9,10},{10,1... | collective-permute-start | bytes 12296 | tf_op jit(solution)/shard_map/ppermute | solution.py:247
  38.8 3.1 %collective-permute-start.2 = (bf16[2,2,8,128]{3,2,0,1:T(8,128)(2,1)S(1)}, bf16[2,2,8,128]{3,2,0,1:T(8,128)(2,1)S(1)}, u32[]{:S(2)}, u32[]{:S(2)}) collective-permute-start(bf16[2,2,8,128]{3,2,0,1:T(8,128)(2,1)S(1)} %get-tuple-element.29), channel_id=1, source_target_pairs={{0,8},{8,0},{16,24},{24,16},{32,40},{40,32},{48,56},{56,48},{64,72... | collective-permute-start | bytes 24584 | tf_op jit(solution)/shard_map/ppermute | solution.py:251
  42.0 2.5 %collective-permute-start.4 = (bf16[4,8,128]{2,1,0:T(8,128)(2,1)S(1)}, bf16[4,8,128]{2,1,0:T(8,128)(2,1)S(1)}, u32[]{:S(2)}, u32[]{:S(2)}) collective-permute-start(bf16[4,8,128]{2,1,0:T(8,128)(2,1)S(1)} %fusion), channel_id=1, source_target_pairs={{0,1},{1,2},{2,3},{3,4},{4,5},{5,6},{6,7},{7,0},{8,15},{9,8},{10,9... | collective-permute-start | bytes 24584 | tf_op jit(solution)/shard_map/ppermute | solution.py:270
  42.0 2.7 %collective-permute-start.3 = (bf16[4,2,8,128]{3,2,0,1:T(8,128)(2,1)S(1)}, bf16[4,2,8,128]{3,2,0,1:T(8,128)(2,1)S(1)}, u32[]{:S(2)}, u32[]{:S(2)}) collective-permute-start(bf16[4,2,8,128]{3,2,0,1:T(8,128)(2,1)S(1)} %constant_dynamic-update-slice_fusion), channel_id=1, source_target_pairs={{0,16},{8,120},{16,32},{24,8},{32,48},{40,24},{48,64},{56,40},{64,... | collective-permute-start | bytes 49160 | tf_op jit(solution)/shard_map/ppermute | solution.py:267
  44.7 5.9 %collective-permute-start.5 = (bf16[2,3,8,128]{3,2,0,1:T(8,128)(2,1)S(1)}, bf16[2,3,8,128]{3,2,0,1:T(8,128)(2,1)S(1)}, u32[]{:S(2)}, u32[]{:S(2)}) collective-permute-start(bf16[2,3,8,128]{3,2,0,1:T(8,128)(2,1)S(1)} %pad_maximum_fusion.1), channel_id=1, source_target_pairs={{0,8},{8,0},{16,24},{24,16},{32,40},{40,32},{48,56},{56,48},{64,72... | collective-permute-start | bytes 36872 | tf_op jit(solution)/shard_map/ppermute | solution.py:251
  50.6 2.3 %copy-start.1 = (bf16[9,2,2,8,64,128]{5,4,3,2,1,0:T(8,128)(2,1)S(1)}, bf16[9,2,2,8,64,128]{5,4,3,2,1,0:T(8,128)(2,1)}, u32[]{:S(2)}) copy-start(bf16[9,2,2,8,64,128]{5,4,3,2,1,0:T(8,128)(2,1)} %links_ref.3) | copy-start | bytes 14155780

commit v2 on v1

--- a/solution.py
+++ b/solution.py
@@ -11,7 +11,8 @@
 BF16 = jnp.bfloat16
 F32 = jnp.float32
 VMEM = pl.BlockSpec(memory_space=pltpu.VMEM)
-LIMIT = 40 * 1024 * 1024
+MIB = 1024 * 1024
+STAGE = 2
 
 
 def iota(shape, dim):
@@ -34,48 +35,55 @@
     return jnp.where(lane < HALF, folded[0], folded[1])
 
 
-def restrict_kernel(field_ref, vectors_ref, send_ref):
-    x = pl.program_id(0)
-    count = pl.num_programs(0)
+def restrict_kernel(
+    field_hbm, vectors_hbm, links_hbm, send_ref, links_ref, field_ref, vectors_ref, field_sem, vectors_sem, links_sem
+):
     half = lax.axis_index("ta") // 8
+    count = field_ref.shape[0]
+    copies = []
+    for x in range(count):
+        copies.append(pltpu.make_async_copy(field_hbm.at[0, x], field_ref.at[x], field_sem.at[x]))
+        copies.append(pltpu.make_async_copy(vectors_hbm.at[0, x], vectors_ref.at[x], vectors_sem.at[x]))
+    links_copy = pltpu.make_async_copy(links_hbm, links_ref, links_sem)
+    for copy in copies + [links_copy]:
+        copy.start()
     even = iota((16, 768), 1) % 2 == 0
-    parts = []
-    for z in range(2):
-        values = field_ref[0, 0, z].astype(F32)
-        values = jnp.concatenate([values[:, 0, :], values[:, 1, :]], axis=0)
-        after = pltpu.roll(values, 767, 1)
-        before = pltpu.roll(values, 1, 1)
-        turned = jnp.where(even, after, -before)
-        rows = jnp.concatenate([values, turned], axis=0).astype(BF16)
-        vectors = vectors_ref[0, 0, z].reshape(512, 768)
-        products = lax.dot_general(
-            rows, vectors, (((1,), (1,)), ((), ())), preferred_element_type=F32
-        )
-        first = iota((8, 512), 1) // 32 % 2 == 0
-        products = jnp.concatenate(
-            [
+    first = iota((8, 512), 1) // 32 % 2 == 0
+    for x in range(count):
+        if x % STAGE == 0:
+            for copy in copies[2 * x : 2 * (x + STAGE)]:
+                copy.wait()
+        parts = []
+        for z in range(2):
+            values = field_ref[x, z].astype(F32)
+            values = jnp.concatenate([values[:, 0, :], values[:, 1, :]], axis=0)
+            turned = jnp.where(even, pltpu.roll(values, 767, 1), -pltpu.roll(values, 1, 1))
+            products = lax.dot_general(
+                jnp.concatenate([values, turned], axis=0).astype(BF16),
+                vectors_ref[x, z].reshape(512, 768),
+                (((1,), (1,)), ((), ())),
+                preferred_element_type=F32,
+            )
+            products = [
                 jnp.where(first, products[o * 16 : o * 16 + 8], products[o * 16 + 8 : o * 16 + 16])
                 for o in range(2)
-            ],
-            axis=0,
-        )
-        parts.append(own_site(products))
-    partial = jnp.stack(parts)
-    high = partial.astype(BF16)
-    low = (partial - high.astype(F32)).astype(BF16)
-    behind = lax.rem(x + count - 1, count)
-    ahead = lax.rem(x + 1, count)
-    send_ref[2 * x + half, 0] = high
-    send_ref[2 * x + half, 1] = low
-    send_ref[2 * x + 1 - half, 0] = high
-    send_ref[2 * x + 1 - half, 1] = low
-    send_ref[2 * behind + half, 2] = high
-    send_ref[2 * ahead + half, 3] = high
-    send_ref[2 * x + 1 - half, 2] = high
-    send_ref[2 * x + 1 - half, 3] = high
-
-
-def gather_kernel(received_ref, source_ref, own_ref, other_ref, plus_ref, minus_ref):
+            ]
+            parts.append(own_site(jnp.concatenate(products, axis=0)))
+        partial = jnp.stack(parts)
+        high = partial.astype(BF16)
+        low = (partial - high.astype(F32)).astype(BF16)
+        send_ref[2 * x + half, 0] = high
+        send_ref[2 * x + half, 1] = low
+        send_ref[2 * x + 1 - half, 0] = high
+        send_ref[2 * x + 1 - half, 1] = low
+        send_ref[2 * ((x - 1) % count) + half, 2] = high
+        send_ref[2 * ((x + 1) % count) + half, 3] = high
+        send_ref[2 * x + 1 - half, 2] = high
+        send_ref[2 * x + 1 - half, 3] = high
+    links_copy.wait()
+
+
+def gather_kernel(received_ref, source_ref, edge_ref, other_ref, plus_ref, minus_ref):
     half = lax.axis_index("ta") % 2
 
     def summed(first, slots):
@@ -91,8 +99,10 @@
 
     source = summed(8 * half, (0, 1))
     source_ref[...] = source
-    own_ref[...] = source.astype(BF16)
-    other_ref[...] = summed(8 - 8 * half, (0, 1)).astype(BF16)
+    other = summed(8 - 8 * half, (0, 1))
+    other_ref[...] = other.astype(BF16)
+    chip = jnp.concatenate([source, other], axis=0)
+    edge_ref[...] = jnp.where(half == 1, chip[:, 0], chip[:, 1]).astype(BF16)
     plus_ref[...] = summed(8 * half, (2,)).astype(BF16)
     minus_ref[...] = summed(8 * half, (3,)).astype(BF16)
 
@@ -143,15 +153,18 @@
     return jnp.stack(plain).reshape(shape), jnp.stack(full).reshape(shape)
 
 
-def first_kernel(links_ref, source_ref, other_ref, plus_ref, minus_ref, up_ref, down_ref, image_ref, full_ref, own_ref):
+def first_kernel(
+    links_ref, source_ref, other_ref, plus_ref, minus_ref, along_z_ref, swapped_ref, image_ref, full_ref, own_ref, _
+):
+    up, down = ordered(along_z_ref[:2], swapped_ref[...])
     image, full = applied(
         links_ref,
         source_ref[...],
         other_ref[...].astype(F32),
         plus_ref[...].astype(F32),
         minus_ref[...].astype(F32),
-        up_ref[...].astype(F32),
-        down_ref[...].astype(F32),
+        up,
+        down,
     )
     image_ref[...] = image
     full_ref[...] = full
@@ -165,17 +178,19 @@
 
 
 def second_kernel(
-    links_ref, source_ref, image_ref, full_ref, other_ref, plus_ref, minus_ref, up_ref, down_ref, twice_ref, sums_ref
+    links_ref, source_ref, image_ref, full_ref, other_ref, along_x_ref, along_z_ref, swapped_ref, twice_ref, sums_ref
 ):
     image = image_ref[...]
+    plus, minus = ordered(along_x_ref[:2], swapped_ref[:, :2])
+    up, down = ordered(along_z_ref[:2], swapped_ref[:, 2])
     _, twice = applied(
         links_ref,
         image,
         other_ref[...].astype(F32),
-        plus_ref[...].astype(F32),
-        minus_ref[...].astype(F32),
-        up_ref[...].astype(F32),
-        down_ref[...].astype(F32),
+        plus,
+        minus,
+        up,
+        down,
     )
     twice_ref[...] = twice
     source = source_ref[...]
@@ -242,11 +257,6 @@
     residual_ref[...] = residual - scaled(beta, second)
 
 
-def shift(block, axis, distance):
-    count = lax.axis_size(axis)
-    return lax.ppermute(block, axis, [(i, (i + distance) % count) for i in range(count)])
-
-
 def from_core(block):
     return lax.ppermute(block, "ta", [(i, i ^ 1) for i in range(lax.axis_size("ta"))])
 
@@ -255,76 +265,109 @@
     return jax.ShapeDtypeStruct(shape, dtype)
 
 
-def params():
-    return pltpu.CompilerParams(vmem_limit_bytes=LIMIT)
-
-
-def halo(own):
+def params(limit=16):
+    return pltpu.CompilerParams(vmem_limit_bytes=limit * MIB)
+
+
+def z_step(block):
     count_ta, count_xyz = lax.axis_size("ta"), lax.axis_size("xyz")
+    route = [
+        (i * count_xyz + j, i * count_xyz + (j + (1 if i % 2 == 0 else -1)) % count_xyz)
+        for i in range(count_ta)
+        for j in range(count_xyz)
+    ]
+    return lax.ppermute(block, ("ta", "xyz"), route)
+
+
+def x_step(block):
+    count = lax.axis_size("ta")
+    return lax.ppermute(block, "ta", [(i, (i + (2 if i % 2 == 0 else -2)) % count) for i in range(count)])
+
+
+def chip_kernel(_, own_ref, other_ref, links_ref, chip_ref, edge_ref):
+    odd = lax.axis_index("ta") % 2 == 1
+    chip_ref[:2] = own_ref[...]
+    chip_ref[2:] = other_ref[...]
+    edge_ref[...] = jnp.where(odd, chip_ref[:, 0].astype(F32), chip_ref[:, 1].astype(F32)).astype(BF16)
+
+
+def swap_kernel(_, along_x_ref, along_z_ref, links_ref, back_ref):
+    back_ref[:, :2] = along_x_ref[2:]
+    back_ref[:, 2] = along_z_ref[2:]
+
+
+def with_links(kernel, links, outs, *args):
+    return pl.pallas_call(
+        kernel,
+        in_specs=[VMEM] * (1 + len(args)),
+        out_specs=[VMEM] * (1 + len(outs)),
+        out_shape=[pltpu.VMEM(links.shape, BF16)] + [struct(*out) for out in outs],
+        input_output_aliases={0: 0},
+        compiler_params=params(),
+        name=kernel.__name__,
+    )(links, *args)
+
+
+def halo(own, links):
     other = from_core(own)
+    links, chip, edge = with_links(chip_kernel, links, [((4, 2, 8, WIDE), BF16), ((4, 8, WIDE), BF16)], own, other)
+    along_x, along_z = x_step(chip), z_step(edge)
+    links, back = with_links(swap_kernel, links, [((2, 3, 8, WIDE), BF16)], along_x, along_z)
+    return links, other, along_x, along_z, from_core(back)
+
+
+def ordered(received, swapped):
     odd = lax.axis_index("ta") % 2 == 1
-    chip = jnp.concatenate([own, other], axis=0)
-    along_x = lax.ppermute(
-        chip, "ta", [(i, (i + (2 if i % 2 == 0 else -2)) % count_ta) for i in range(count_ta)]
-    )
-    along_z = lax.ppermute(
-        jnp.where(odd, chip[:, 0], chip[:, 1]),
-        ("ta", "xyz"),
-        [
-            (i * count_xyz + j, i * count_xyz + (j + (1 if i % 2 == 0 else -1)) % count_xyz)
-            for i in range(count_ta)
-            for j in range(count_xyz)
-        ],
-    )
-    back = jnp.concatenate([along_x[2:], along_z[2:, None]], axis=1)
-    swapped = from_core(back)
-    mine = jnp.concatenate([along_x[:2], along_z[:2, None]], axis=1)
-    plus = jnp.where(odd, mine, swapped)
-    minus = jnp.where(odd, swapped, mine)
-    return other, plus[:, :2], minus[:, :2], plus[:, 2], minus[:, 2]
+    received, swapped = received.astype(F32), swapped.astype(F32)
+    return jnp.where(odd, received, swapped), jnp.where(odd, swapped, received)
 
 
 def on_device(fine_field, null_vectors, coarse_links):
     field4 = (2, 2, 8, WIDE)
-    send = pl.pallas_call(
+    send, links = pl.pallas_call(
         restrict_kernel,
-        grid=(8,),
-        in_specs=[
-            pl.BlockSpec((1, 1, 2, 8, 2, 768), lambda x: (0, x, 0, 0, 0, 0)),
-            pl.BlockSpec((1, 1, 2, 8, 2, 32, 768), lambda x: (0, x, 0, 0, 0, 0, 0)),
+        in_specs=[pl.BlockSpec(memory_space=pltpu.HBM)] * 3,
+        out_specs=[VMEM] * 2,
+        out_shape=[struct((16, 4, 2, 8, WIDE), BF16), pltpu.VMEM(coarse_links.shape, BF16)],
+        scratch_shapes=[
+            pltpu.VMEM(fine_field.shape[1:], BF16),
+            pltpu.VMEM(null_vectors.shape[1:], BF16),
+            pltpu.SemaphoreType.DMA((8,)),
+            pltpu.SemaphoreType.DMA((8,)),
+            pltpu.SemaphoreType.DMA,
         ],
-        out_specs=pl.BlockSpec((16, 4, 2, 8, WIDE), lambda x: (0, 0, 0, 0, 0)),
-        out_shape=struct((16, 4, 2, 8, WIDE), BF16),
-        compiler_params=params(),
+        compiler_params=params(32),
         name="restrict",
-    )(fine_field, null_vectors)
+    )(*(pltpu.with_memory_space_constraint(v, pltpu.HBM) for v in (fine_field, null_vectors, coarse_links)))
     received = lax.all_to_all(send, "ta", 0, 0)
-    source, own, other, plus, minus = pl.pallas_call(
+    source, edge, other, plus, minus = pl.pallas_call(
         gather_kernel,
         in_specs=[VMEM],
         out_specs=[VMEM] * 5,
-        out_shape=[struct(field4)] + [struct(field4, BF16)] * 4,
+        out_shape=[struct(field4), struct((4, 8, WIDE), BF16)] + [struct(field4, BF16)] * 3,
         compiler_params=params(),
         name="gather",
     )(received)
-    down = shift(own[:, 1], "xyz", 1)
-    up = shift(own[:, 0], "xyz", -1)
-    image, full, own = pl.pallas_call(
+    along_z = z_step(edge)
+    swapped = from_core(along_z[2:])
+    image, full, own, links = pl.pallas_call(
         first_kernel,
         in_specs=[VMEM] * 7,
-        out_specs=[VMEM] * 3,
-        out_shape=[struct(field4), struct(field4), struct(field4, BF16)],
+        out_specs=[VMEM] * 4,
+        out_shape=[struct(field4), struct(field4), struct(field4, BF16), pltpu.VMEM(links.shape, BF16)],
+        input_output_aliases={0: 3},
         compiler_params=params(),
         name="first",
-    )(coarse_links, source, other, plus, minus, up, down)
+    )(links, source, other, plus, minus, along_z, swapped)
+    links, *around = halo(own, links)
     twice, sums = pl.pallas_call(
         second_kernel,
-        in_specs=[VMEM] * 9,
+        in_specs=[VMEM] * 8,
         out_specs=[VMEM] * 2,
         out_shape=[struct(field4), struct((128, 1, WIDE))],
         compiler_params=params(),
         name="second",
-    )(coarse_links, source, image, full, *halo(own))
+    )(pltpu.with_memory_space_constraint(links, pltpu.VMEM), source, image, full, *around)
     sums = lax.all_to_all(sums, ("ta", "xyz"), 0, 0)
     return pl.pallas_call(
         last_kernel,

time: 70.5 us -> 61.2 us (0.87)
  local copies, waits for them, and re-layouts: 7.95 us -> 0.01 us
  waiting for transfers between devices: 10.2 us -> 4.07 us
  blocking collectives: 28.8 us -> 30.7 us
  starting transfers between devices: 13.2 us -> 14.8 us
  Pallas kernels: 9.41 us -> 10.8 us
    unnamed x9 -> x0, local copies, waits for them, and re-layouts: 7.92 us -> none
    ppermute x4 -> x3, waiting for transfers between devices: 8.52 us -> 1.59 us  [the longest x2 1.59 us: z_step(): return lax.ppermute(block, ('ta', 'xyz'), route)]
    ppermute x4 -> x3, starting transfers between devices: 5.8 us -> 10.6 us  [the longest x2 10 us: z_step(): return lax.ppermute(block, ('ta', 'xyz'), route)]
    ppermute x2 -> x3, starting transfers between devices: 7.39 us -> 4.16 us  [from_core(): lax.ppermute(block, 'ta', [(i, i ^ 1) for i in range(lax.axis_size('ta'))])]
    all_to_all x1, blocking collectives: 14.5 us -> 16.4 us  [on_device(): sums = lax.all_to_all(sums, ('ta', 'xyz'), 0, 0)]
    pallas_call x3 -> x5, Pallas kernels: 8.24 us -> 9.66 us  [the longest x1 6.52 us: on_device(): pl.pallas_call(restrict_kernel, in_specs=[pl.BlockSpec(memory_space=pltpu...]
    ppermute x2 -> x3, waiting for transfers between devices: 1.66 us -> 2.49 us  [from_core(): lax.ppermute(block, 'ta', [(i, i ^ 1) for i in range(lax.axis_size('ta'))])]
  transfers between devices with their start and end apart: 6 -> 6, of which waited for: 6 -> 5; matrix products, arithmetic and copies ran while one was open for 0% -> 0% of each run, Pallas kernels for 0% -> 0%
where the time goes in v2:
time: 61.2 us; the launch traced here: 61 us
  blocking collectives  30.7 us (50%)
  starting transfers between devices  14.8 us (24%)
  Pallas kernels  10.8 us (18%)
  waiting for transfers between devices  4.07 us (7%)
  between operations  0.66 us (1%)
    all_to_all x1, blocking collectives, on_device(): sums = lax.all_to_all(sums, ('ta', 'xyz'), 0, 0)  16.4 us
    all_to_all x1, blocking collectives, on_device(): received = lax.all_to_all(send, 'ta', 0, 0)  14.3 us
    ppermute x2, starting transfers between devices, z_step(): return lax.ppermute(block, ('ta', 'xyz'), route)  10 us
    pallas_call x1, Pallas kernels, on_device(): pl.pallas_call(restrict_kernel, in_specs=[pl.BlockSpec(memory_space=pltpu...  6.52 us
    ppermute x3, starting transfers between devices, from_core(): lax.ppermute(block, 'ta', [(i, i ^ 1) for i in range(lax.axis_size('ta'))])  4.16 us
    ppermute x3, waiting for transfers between devices, from_core(): lax.ppermute(block, 'ta', [(i, i ^ 1) for i in range(lax.axis_size('ta'))])  2.49 us
    pallas_call x1, Pallas kernels, on_device(): pl.pallas_call(second_kernel, in_specs=[VMEM] * 8, out_specs=[VMEM] * 2,...  1.67 us
    ppermute x2, waiting for transfers between devices, z_step(): return lax.ppermute(block, ('ta', 'xyz'), route)  1.59 us
  transfers between devices with their start and end apart: 6, of which 5 were waited for; matrix products, arithmetic and copies ran while one was open for 0% of the time, Pallas kernels for 0%

profile of v2, /device:TPU:1, one launch (start us, length us, event | category | flops | bytes accessed | tf_op | source)
XLA Modules:
  0.0 61.0 jit_solution(10037647075345467038)
XLA Ops:
  0.6 6.5 %restrict.1 = (bf16[16,4,2,8,128]{4,3,2,1,0:T(8,128)(2,1)S(1)}, bf16[9,2,2,8,64,128]{5,4,3,2,1,0:T(8,128)(2,1)S(1)}) custom-call(bf16[1,8,2,8,2,768]{5,4,3,2,1,0:T(2,128)(2,1)} %field_hbm.1, bf16[1,8,2,8,2,32,768]{6,5,4,3,2,1,0:T(8,128)(2,1)} %vectors_hbm.1, bf16[9,2,2,8,64,128]{5,4,3,2,1,0:T(8,128)(2,1)} %links_hbm.1), custom_call_target="tpu_custom_call" | custom-call | tf_op jit(solution)/shard_map/restrict/pallas_call | solution.py:327
  7.2 14.3 %all_to_all.10.received_ref = bf16[16,4,2,8,128]{4,3,2,1,0:T(8,128)(2,1)S(1)} all-to-all(bf16[16,4,2,8,128]{4,3,2,1,0:T(8,128)(2,1)S(1)} %get-tuple-element.21), channel_id=1, replica_groups=mesh['ta'=16,'xyz'=8] {'ta'}, dimensions={0} | all-to-all | bytes 524288 | tf_op jit(solution)/shard_map/all_to_all | solution.py:342
  21.5 5.6 %collective-permute-start = (bf16[4,8,128]{2,1,0:T(8,128)(2,1)S(1)}, bf16[4,8,128]{2,1,0:T(8,128)(2,1)S(1)}, u32[]{:S(2)}, u32[]{:S(2)}) collective-permute-start(bf16[4,8,128]{2,1,0:T(8,128)(2,1)S(1)} %get-tuple-element.26), channel_id=1, source_target_pairs={{0,1},{1,2},{2,3},{3,4},{4,5},{5,6},{6,7},{7,0},{8,15},{9,8},{10,9... | collective-permute-start | bytes 24584 | tf_op jit(solution)/shard_map/ppermute | solution.py:279
  27.1 0.8 %collective-permute-done.along_z_ref = bf16[4,8,128]{2,1,0:T(8,128)(2,1)S(1)} collective-permute-done((bf16[4,8,128]{2,1,0:T(8,128)(2,1)S(1)}, bf16[4,8,128]{2,1,0:T(8,128)(2,1)S(1)}, u32[]{:S(2)}, u32[]{:S(2)}) %collective-permute-start) | collective-permute-done | bytes 8224 | tf_op jit(solution)/shard_map/ppermute | solution.py:279
  27.9 1.9 %collective-permute-start.1 = (bf16[2,8,128]{2,1,0:T(8,128)(2,1)S(1)}, bf16[2,8,128]{2,1,0:T(8,128)(2,1)S(1)}, u32[]{:S(2)}, u32[]{:S(2)}) collective-permute-start(bf16[2,8,128]{2,1,0:T(8,128)(2,1)S(1)} %slice.4), channel_id=1, source_target_pairs={{0,8},{8,0},{16,24},{24,16},{32,40},{40,32},{48,56},{56,48},{64,72... | collective-permute-start | bytes 12296 | tf_op jit(solution)/shard_map/ppermute | solution.py:261
  29.8 0.8 %collective-permute-done.1.swapped_ref = bf16[2,8,128]{2,1,0:T(8,128)(2,1)S(1)} collective-permute-done((bf16[2,8,128]{2,1,0:T(8,128)(2,1)S(1)}, bf16[2,8,128]{2,1,0:T(8,128)(2,1)S(1)}, u32[]{:S(2)}, u32[]{:S(2)}) %collective-permute-start.1) | collective-permute-done | bytes 4128 | tf_op jit(solution)/shard_map/ppermute | solution.py:261
  30.6 1.5 %first.1 = (f32[2,2,8,128]{3,2,1,0:T(8,128)S(1)}, f32[2,2,8,128]{3,2,1,0:T(8,128)S(1)}, bf16[2,2,8,128]{3,2,1,0:T(8,128)(2,1)S(1)}, bf16[9,2,2,8,64,128]{5,4,3,2,1,0:T(8,128)(2,1)S(1)}) custom-call(bf16[9,2,2,8,64,128]{5,4,3,2,1,0:T(8,128)(2,1)S(1)} %get-tuple-element.20.links_ref, ...), custom_call_target="tpu_custom_call", output_to_operand_aliasing={{3}: (0, {})} | custom-call | tf_op jit(solution)/shard_map/first/pallas_call | solution.py:353
  32.1 0.4 collective-permute-start.2
  32.5 0.8 %collective-permute-done.2.other_ref = bf16[2,2,8,128]{3,2,1,0:T(8,128)(2,1)S(1)} collective-permute-done((bf16[2,2,8,128]{3,2,1,0:T(8,128)(2,1)S(1)}, bf16[2,2,8,128]{3,2,1,0:T(8,128)(2,1)S(1)}, u32[]{:S(2)}, u32[]{:S(2)}) %collective-permute-start.2) | collective-permute-done | bytes 8224 | tf_op jit(solution)/shard_map/ppermute | solution.py:261
  33.3 0.6 collective-permute-start.3
  33.9 4.4 %collective-permute-start.4 = (bf16[4,8,128]{2,1,0:T(8,128)(2,1)S(1)}, bf16[4,8,128]{2,1,0:T(8,128)(2,1)S(1)}, u32[]{:S(2)}, u32[]{:S(2)}) collective-permute-start(bf16[4,8,128]{2,1,0:T(8,128)(2,1)S(1)} %get-tuple-element.31), channel_id=1, source_target_pairs={{0,1},{1,2},{2,3},{3,4},{4,5},{5,6},{6,7},{7,0},{8,15},{9,8},{10,9... | collective-permute-start | bytes 24584 | tf_op jit(solution)/shard_map/ppermute | solution.py:279
  38.3 0.8 %collective-permute-done.4.along_z_ref = bf16[4,8,128]{2,1,0:T(8,128)(2,1)S(1)} collective-permute-done((bf16[4,8,128]{2,1,0:T(8,128)(2,1)S(1)}, bf16[4,8,128]{2,1,0:T(8,128)(2,1)S(1)}, u32[]{:S(2)}, u32[]{:S(2)}) %collective-permute-start.4) | collective-permute-done | bytes 8224 | tf_op jit(solution)/shard_map/ppermute | solution.py:279
  39.1 0.0 collective-permute-done.3.along_x_ref
  39.1 1.9 %collective-permute-start.5 = (bf16[2,3,8,128]{3,2,1,0:T(8,128)(2,1)S(1)}, bf16[2,3,8,128]{3,2,1,0:T(8,128)(2,1)S(1)}, u32[]{:S(2)}, u32[]{:S(2)}) collective-permute-start(bf16[2,3,8,128]{3,2,1,0:T(8,128)(2,1)S(1)} %get-tuple-element.35), channel_id=1, source_target_pairs={{0,8},{8,0},{16,24},{24,16},{32,40},{40,32},{48,56},{56,48},{64,72... | collective-permute-start | bytes 36872 | tf_op jit(solution)/shard_map/ppermute | solution.py:261
  41.0 0.8 %collective-permute-done.5.swapped_ref = bf16[2,3,8,128]{3,2,1,0:T(8,128)(2,1)S(1)} collective-permute-done((bf16[2,3,8,128]{3,2,1,0:T(8,128)(2,1)S(1)}, bf16[2,3,8,128]{3,2,1,0:T(8,128)(2,1)S(1)}, u32[]{:S(2)}, u32[]{:S(2)}) %collective-permute-start.5) | collective-permute-done | bytes 12320 | tf_op jit(solution)/shard_map/ppermute | solution.py:261
  41.8 1.7 %second.1 = (f32[2,2,8,128]{3,2,1,0:T(8,128)S(1)}, f32[128,1,128]{2,1,0:T(1,128)S(1)}) custom-call(bf16[9,2,2,8,64,128]{5,4,3,2,1,0:T(8,128)(2,1)S(1)} %get-tuple-element.32.links_ref, f32[2,2,8,128]{3,2,1,0:T(8,128)S(1)} %get-tuple-element.22.source_ref, f32[2,2,8,128]{3,2,1,0:T(8,128)S(1)} %get-tuple-element.33.image_ref, ...), custom_call_target="tpu_custom_call" | custom-call | tf_op jit(solution)/shard_map/second/pallas_call | solution.py:363
  43.5 16.4 %all_to_all.11.sums_ref = f32[128,1,128]{2,1,0:T(1,128)S(1)} all-to-all(f32[128,1,128]{2,1,0:T(1,128)S(1)} %get-tuple-element.36), channel_id=1, replica_groups=mesh['ta'=16,'xyz'=8] {'ta','xyz'}, dimensions={0} | all-to-all | bytes 131072 | tf_op jit(solution)/shard_map/all_to_all | solution.py:371
  59.9 1.1 %last.1 = (f32[2,2,8,128]{3,2,1,0:T(8,128)}, f32[2,2,8,128]{3,2,1,0:T(8,128)}) custom-call(f32[128,1,128]{2,1,0:T(1,128)S(1)} %all_to_all.11.sums_ref, f32[2,2,8,128]{3,2,1,0:T(8,128)S(1)} %get-tuple-element.22.source_ref, f32[2,2,8,128]{3,2,1,0:T(8,128)S(1)} %get-tuple-element.33.image_ref, f32[2,2,8,128]{3,2,1,0:T(8,128)S(1)} %get-tuple-element.34.full_ref, ...), custom_call_target="tpu_custom_call" | custom-call | tf_op jit(solution)/shard_map/last/pallas_call | solution.py:372
  (4 shorter events, 0.0 us)
Async XLA Ops:
  21.5 6.4 %collective-permute-start = (bf16[4,8,128]{2,1,0:T(8,128)(2,1)S(1)}, bf16[4,8,128]{2,1,0:T(8,128)(2,1)S(1)}, u32[]{:S(2)}, u32[]{:S(2)}) collective-permute-start(bf16[4,8,128]{2,1,0:T(8,128)(2,1)S(1)} %get-tuple-element.26), channel_id=1, source_target_pairs={{0,1},{1,2},{2,3},{3,4},{4,5},{5,6},{6,7},{7,0},{8,15},{9,8},{10,9... | collective-permute-start | bytes 24584 | tf_op jit(solution)/shard_map/ppermute | solution.py:279
  27.9 2.7 %collective-permute-start.1 = (bf16[2,8,128]{2,1,0:T(8,128)(2,1)S(1)}, bf16[2,8,128]{2,1,0:T(8,128)(2,1)S(1)}, u32[]{:S(2)}, u32[]{:S(2)}) collective-permute-start(bf16[2,8,128]{2,1,0:T(8,128)(2,1)S(1)} %slice.4), channel_id=1, source_target_pairs={{0,8},{8,0},{16,24},{24,16},{32,40},{40,32},{48,56},{56,48},{64,72... | collective-permute-start | bytes 12296 | tf_op jit(solution)/shard_map/ppermute | solution.py:261
  32.1 1.2 %collective-permute-start.2 = (bf16[2,2,8,128]{3,2,1,0:T(8,128)(2,1)S(1)}, bf16[2,2,8,128]{3,2,1,0:T(8,128)(2,1)S(1)}, u32[]{:S(2)}, u32[]{:S(2)}) collective-permute-start(bf16[2,2,8,128]{3,2,1,0:T(8,128)(2,1)S(1)} %get-tuple-element.28.own_ref), channel_id=1, source_target_pairs={{0,8},{8,0},{16,24},{24,16},{32,40},{40,32},{48,56},{56,48},{64,72... | collective-permute-start | bytes 24584 | tf_op jit(solution)/shard_map/ppermute | solution.py:261
  33.3 5.8 %collective-permute-start.3 = (bf16[4,2,8,128]{3,2,1,0:T(8,128)(2,1)S(1)}, bf16[4,2,8,128]{3,2,1,0:T(8,128)(2,1)S(1)}, u32[]{:S(2)}, u32[]{:S(2)}) collective-permute-start(bf16[4,2,8,128]{3,2,1,0:T(8,128)(2,1)S(1)} %get-tuple-element.30), channel_id=1, source_target_pairs={{0,16},{8,120},{16,32},{24,8},{32,48},{40,24},{48,64},{56,40},{64,... | collective-permute-start | bytes 49160 | tf_op jit(solution)/shard_map/ppermute | solution.py:284
  33.9 5.2 %collective-permute-start.4 = (bf16[4,8,128]{2,1,0:T(8,128)(2,1)S(1)}, bf16[4,8,128]{2,1,0:T(8,128)(2,1)S(1)}, u32[]{:S(2)}, u32[]{:S(2)}) collective-permute-start(bf16[4,8,128]{2,1,0:T(8,128)(2,1)S(1)} %get-tuple-element.31), channel_id=1, source_target_pairs={{0,1},{1,2},{2,3},{3,4},{4,5},{5,6},{6,7},{7,0},{8,15},{9,8},{10,9... | collective-permute-start | bytes 24584 | tf_op jit(solution)/shard_map/ppermute | solution.py:279
  39.1 2.7 %collective-permute-start.5 = (bf16[2,3,8,128]{3,2,1,0:T(8,128)(2,1)S(1)}, bf16[2,3,8,128]{3,2,1,0:T(8,128)(2,1)S(1)}, u32[]{:S(2)}, u32[]{:S(2)}) collective-permute-start(bf16[2,3,8,128]{3,2,1,0:T(8,128)(2,1)S(1)} %get-tuple-element.35), channel_id=1, source_target_pairs={{0,8},{8,0},{16,24},{24,16},{32,40},{40,32},{48,56},{56,48},{64,72... | collective-permute-start | bytes 36872 | tf_op jit(solution)/shard_map/ppermute | solution.py:261

commit v3 on v0

v3 whole, which is shorter than its diff:
```python
import jax
import jax.numpy as jnp
from jax import lax
from jax.experimental import pallas as pl
from jax.experimental.pallas import tpu as pltpu
from jax.sharding import PartitionSpec as P

TSPAN = 4
HALF = 64
WIDE = 128
BF16 = jnp.bfloat16
F32 = jnp.float32
VMEM = pl.BlockSpec(memory_space=pltpu.VMEM)
MIB = 1024 * 1024
STAGE = 2
EDGE = 12


def iota(shape, dim):
    return lax.broadcasted_iota(jnp.int32, shape, dim)


def halves_swapped(values):
    return pltpu.roll(values, HALF, values.ndim - 1)


def own_site(products):
    folded = []
    row, lane = iota((8, WIDE), 0), iota((8, WIDE), 1)
    for o in range(2):
        total = jnp.zeros((8, WIDE), F32)
        for pair in range(4):
            block = products[o * 8 : o * 8 + 8, pair * WIDE : (pair + 1) * WIDE]
            total = total + jnp.where(row == 2 * pair + lane // HALF, block, 0.0)
        folded.append(total + halves_swapped(total))
    return jnp.where(lane < HALF, folded[0], folded[1])


def restrict_kernel(
    field_hbm, vectors_hbm, send_ref, field_ref, vectors_ref, products_ref, field_sem, vectors_sem
):
    count = field_ref.shape[0]
    copies = []
    for x in range(count):
        copies.append(pltpu.make_async_copy(field_hbm.at[0, x], field_ref.at[x], field_sem.at[x]))
        copies.append(pltpu.make_async_copy(vectors_hbm.at[0, x], vectors_ref.at[x], vectors_sem.at[x]))
    for copy in copies:
        copy.start()
    even = iota((16, 768), 1) % 2 == 0
    first = iota((8, 512), 1) // 32 % 2 == 0

    def multiply(x, z):
        values = field_ref[x, z].astype(F32)
        values = jnp.concatenate([values[:, 0, :], values[:, 1, :]], axis=0)
        turned = jnp.where(even, pltpu.roll(values, 767, 1), -pltpu.roll(values, 1, 1))
        products_ref[x, z] = lax.dot_general(
            jnp.concatenate([values, turned], axis=0).astype(BF16),
            vectors_ref[x, z].reshape(512, 768),
            (((1,), (1,)), ((), ())),
            preferred_element_type=F32,
        )

    def finish(x, z):
        products = products_ref[x, z]
        products = [
            jnp.where(first, products[o * 16 : o * 16 + 8], products[o * 16 + 8 : o * 16 + 16])
            for o in range(2)
        ]
        partial = own_site(jnp.concatenate(products, axis=0))
        send_ref[2 * x, z] = partial
        send_ref[2 * x + 1, z] = partial

    for stage in range(0, count + STAGE, STAGE):
        if stage < count:
            for copy in copies[2 * stage : 2 * (stage + STAGE)]:
                copy.wait()
        for x in range(stage, stage + STAGE):
            for z in range(2):
                if x < count:
                    multiply(x, z)
                if x >= STAGE:
                    finish(x - STAGE, z)


def edge_of(chip):
    plane = jnp.where(lax.axis_index("ta") % 2 == 1, chip[:, 0], chip[:, 1])
    return jnp.concatenate([plane, jnp.zeros((EDGE - 4,) + plane.shape[1:], F32)], axis=0).astype(BF16)


def gather_kernel(received_ref, source_ref, other_ref, chip_ref, edge_ref):
    half = lax.axis_index("ta") % 2

    def summed(first):
        rows = []
        for s in range(2):
            terms = [received_ref[first + s * TSPAN + i] for i in range(TSPAN)]
            rows.append((terms[0] + terms[1]) + (terms[2] + terms[3]))
        return jnp.stack(rows)

    source, other = summed(8 * half), summed(8 - 8 * half)
    chip = jnp.concatenate([source, other], axis=0)
    source_ref[...] = source
    other_ref[...] = other.astype(BF16)
    chip_ref[...] = chip.astype(BF16)
    edge_ref[...] = edge_of(chip)


def forms(v):
    lane = iota((8, WIDE), 1)
    return jnp.concatenate([jnp.where(lane < HALF, v, -v), halves_swapped(v)], axis=0).astype(BF16)


def hops(links_ref, r, z, terms):
    total = None
    for i in range(0, len(terms), 2):
        pair = terms[i : i + 2]
        product = lax.dot_general(
            jnp.concatenate([forms(v) for _, v in pair], axis=1),
            jnp.concatenate([links_ref[d, r, z].reshape(512, WIDE) for d, _ in pair], axis=1),
            (((1,), (1,)), ((), ())),
            preferred_element_type=F32,
        )
        total = product if total is None else total + product
    return total


def applied_here(links_ref, own, other, r):
    rounded = own.astype(BF16).astype(F32)
    low = own - rounded
    plain, lower = [], []
    for z in range(2):
        here = rounded[r, z]
        total = lax.dot_general(
            jnp.concatenate([forms(here), forms(low[r, z])], axis=0),
            links_ref[0, r, z].reshape(512, WIDE),
            (((1,), (1,)), ((), ())),
            preferred_element_type=F32,
        )
        terms = [
            (3, pltpu.roll(here, 7, 0)),
            (4, pltpu.roll(here, 1, 0)),
            (5, rounded[r, 1]) if z == 0 else (6, rounded[r, 0]),
            (7, rounded[1, z] if r == 0 else other[0, z]),
            (8, other[1, z] if r == 0 else rounded[0, z]),
        ]
        plain.append(own_site(total[:16] + hops(links_ref, r, z, terms)))
        lower.append(own_site(total[16:]))
    return jnp.stack(plain), jnp.stack(lower)


def applied_beyond(links_ref, along_x, step_x, along_z, step_z, edge, add):
    for r in range(2):
        for z, terms in (
            (edge, [(step_x, along_x(r, edge)), (step_z, along_z(r))]),
            (1 - edge, [(step_x, along_x(r, 1 - edge))]),
        ):
            add(r, z, own_site(hops(links_ref, r, z, [(d, v.astype(F32)) for d, v in terms])))


def first_here_kernel(links_hbm, source_ref, other_ref, links_ref, plain_ref, lower_ref, links_sem):
    copies = [
        [pltpu.make_async_copy(links_hbm.at[d, r], links_ref.at[d, r], links_sem.at[d, r]) for d in range(9)]
        for r in range(2)
    ]
    here = (0, 3, 4, 5, 6, 7, 8)
    for r in range(2):
        for d in here:
            copies[r][d].start()
    for r in range(2):
        for d in (1, 2):
            copies[r][d].start()
    source, other = source_ref[...], other_ref[...].astype(F32)
    for r in range(2):
        for d in here:
            copies[r][d].wait()
        plain_ref[r], lower_ref[r] = applied_here(links_ref, source, other, r)
    for r in range(2):
        for d in (1, 2):
            copies[r][d].wait()


def near_kernel(links_ref, here_ref, along_x_ref, along_z_ref, _, near_ref):
    odd = lax.axis_index("ta") % 2

    def add(r, z, value):
        near_ref[r, z] = here_ref[r, z] + value

    applied_beyond(
        links_ref, lambda r, z: along_x_ref[r, z], 2 - odd, lambda r: along_z_ref[r], 6 - odd, odd, add
    )


def far(links_ref, near_ref, swapped_ref, total_ref):
    odd = lax.axis_index("ta") % 2

    def add(r, z, value):
        total_ref[r, z] = near_ref[r, z] + value

    applied_beyond(
        links_ref, lambda r, z: swapped_ref[r, z], 1 + odd, lambda r: swapped_ref[r, 2], 5 + odd, 1 - odd, add
    )


def first_far_kernel(links_ref, near_ref, lower_ref, swapped_ref, _, image_ref, full_ref, own_ref):
    far(links_ref, near_ref, swapped_ref, image_ref)
    image = image_ref[...]
    full_ref[...] = image + lower_ref[...]
    own_ref[...] = image.astype(BF16)


def chip_kernel(_, own_ref, other_ref, links_ref, chip_ref, edge_ref):
    chip_ref[:2] = own_ref[...]
    chip_ref[2:] = other_ref[...]
    edge_ref[...] = edge_of(chip_ref[...].astype(F32))


def swap_kernel(_, along_x_ref, along_z_ref, links_ref, back_ref):
    back_ref[:, :2] = along_x_ref[2:]
    back_ref[:, 2] = along_z_ref[2:4]


def turned_back(values):
    lane = iota(values.shape, values.ndim - 1)
    swapped = halves_swapped(values)
    return jnp.where(lane < HALF, swapped, -swapped)


def sum_rows(pairs, norms):
    products = []
    for a, b in pairs:
        products += [a * b, a * turned_back(b)]
    products += [a * a for a in norms]
    return [jnp.sum(v.reshape(32, WIDE), axis=0, keepdims=True) for v in products]


def second_here_kernel(links_ref, image_ref, other_ref, source_ref, full_ref, _, here_ref, rows_ref):
    image, other = image_ref[...], other_ref[...].astype(F32)
    for r in range(2):
        plain, lower = applied_here(links_ref, image, other, r)
        here_ref[r] = plain + lower
    source, full = source_ref[...], full_ref[...]
    rows = sum_rows(((image, source), (full, source), (full, image)), (image, full))
    rows_ref[...] = jnp.concatenate(rows, axis=0)


def second_far_kernel(
    links_ref, near_ref, swapped_ref, source_ref, image_ref, full_ref, rows_ref, twice_ref, sums_ref
):
    far(links_ref, near_ref, swapped_ref, twice_ref)
    twice = twice_ref[...]
    rows = sum_rows(((twice, source_ref[...]), (twice, image_ref[...]), (full_ref[...], twice)), (twice,))
    rows = jnp.concatenate([rows_ref[...]] + rows + [jnp.zeros((1, WIDE), F32)], axis=0)
    sums = jnp.sum(rows, axis=1, keepdims=True)
    line = jnp.sum(
        jnp.where(iota((16, WIDE), 0) == iota((16, WIDE), 1), sums, 0.0), axis=0, keepdims=True
    )
    sums_ref[...] = jnp.broadcast_to(line.reshape(1, 1, WIDE), sums_ref.shape)


def last_kernel(sums_ref, source_ref, image_ref, full_ref, twice_ref, solution_ref, residual_ref):
    line = jnp.sum(jnp.sum(sums_ref[...].reshape(16, 8, WIDE), axis=0), axis=0, keepdims=True)

    def at(k):
        return jnp.broadcast_to(line[:, k : k + 1], (8, WIDE))

    def times(a, b):
        return a[0] * b[0] - a[1] * b[1], a[0] * b[1] + a[1] * b[0]

    image_source, full_source, full_image, twice_source, twice_image, full_twice = (
        (at(k), at(k + 1)) for k in (0, 2, 4, 8, 10, 12)
    )
    image_norm, full_norm, twice_norm = at(6), at(7), at(14)
    alpha = image_source[0] / image_norm, image_source[1] / image_norm
    conj = alpha[0], -alpha[1]
    size = alpha[0] * alpha[0] + alpha[1] * alpha[1]
    term_a = times(alpha, full_image)
    term_b = times(conj, twice_source)
    dot = (
        full_source[0] - term_a[0] - term_b[0] + size * twice_image[0],
        full_source[1] - term_a[1] - term_b[1] + size * twice_image[1],
    )
    norm = full_norm - 2.0 * times(alpha, full_twice)[0] + size * twice_norm
    beta = dot[0] / norm, dot[1] / norm

    def scaled(a, values):
        return a[0] * values - a[1] * turned_back(values)

    source = source_ref[...]
    residual = source - scaled(alpha, image_ref[...])
    second = full_ref[...] - scaled(alpha, twice_ref[...])
    solution_ref[...] = scaled(alpha, source) + scaled(beta, residual)
    residual_ref[...] = residual - scaled(beta, second)


def from_core(block):
    return lax.ppermute(block, "ta", [(i, i ^ 1) for i in range(lax.axis_size("ta"))])


def struct(shape, dtype=F32):
    return jax.ShapeDtypeStruct(shape, dtype)


def z_step(block):
    count_ta, count_xyz = lax.axis_size("ta"), lax.axis_size("xyz")
    route = [
        (i * count_xyz + j, i * count_xyz + (j + (1 if i % 2 == 0 else -1)) % count_xyz)
        for i in range(count_ta)
        for j in range(count_xyz)
    ]
    return lax.ppermute(block, ("ta", "xyz"), route)


def x_step(block):
    count = lax.axis_size("ta")
    return lax.ppermute(block, "ta", [(i, (i + (2 if i % 2 == 0 else -2)) % count) for i in range(count)])


def call(kernel, outs, *args, limit=16, aliases=(), scratch=(), specs=None):
    return pl.pallas_call(
        kernel,
        in_specs=specs or [VMEM] * len(args),
        out_specs=[VMEM] * len(outs),
        out_shape=outs,
        input_output_aliases=dict(aliases),
        scratch_shapes=scratch,
        compiler_params=pltpu.CompilerParams(vmem_limit_bytes=limit * MIB),
        name=kernel.__name__,
    )(*args)


def in_hbm(array):
    return pltpu.with_memory_space_constraint(array, pltpu.HBM)


def on_device(fine_field, null_vectors, coarse_links):
    hbm = pl.BlockSpec(memory_space=pltpu.HBM)
    site = (2, 2, 8, WIDE)
    field, coarse = struct(site), struct(site, BF16)
    chip_rows, edge_rows = struct((4, 2, 8, WIDE), BF16), struct((EDGE, 8, WIDE), BF16)
    back_rows = struct((2, 3, 8, WIDE), BF16)
    held = pltpu.VMEM(coarse_links.shape, BF16)
    through = ((0, 0),)

    (send,) = call(
        restrict_kernel,
        [struct((16, 2, 8, WIDE))],
        in_hbm(fine_field),
        in_hbm(null_vectors),
        limit=32,
        specs=[hbm] * 2,
        scratch=[
            pltpu.VMEM(fine_field.shape[1:], BF16),
            pltpu.VMEM(null_vectors.shape[1:], BF16),
            pltpu.VMEM((8, 2, 32, 512), F32),
            pltpu.SemaphoreType.DMA((8,)),
            pltpu.SemaphoreType.DMA((8,)),
        ],
    )
    received = lax.all_to_all(send, "ta", 0, 0)
    source, other, chip, edge = call(gather_kernel, [field, coarse, chip_rows, edge_rows], received)

    along_x, along_z = x_step(chip), z_step(edge)
    links, plain, lower = call(
        first_here_kernel,
        [held, field, field],
        in_hbm(coarse_links),
        source,
        other,
        specs=[hbm, VMEM, VMEM],
        scratch=[pltpu.SemaphoreType.DMA((9, 2))],
    )
    links, back = call(swap_kernel, [held, back_rows], links, along_x, along_z, aliases=through)
    swapped = from_core(back)
    links, near = call(near_kernel, [held, field], links, plain, along_x, along_z, aliases=through)
    links, image, full, own = call(
        first_far_kernel, [held, field, field, coarse], links, near, lower, swapped, aliases=through
    )

    other = from_core(own)
    links, chip, edge = call(chip_kernel, [held, chip_rows, edge_rows], links, own, other, aliases=through)
    along_x, along_z = x_step(chip), z_step(edge)
    links, here, rows = call(
        second_here_kernel, [held, field, struct((8, WIDE))], links, image, other, source, full, aliases=through
    )
    links, back = call(swap_kernel, [held, back_rows], links, along_x, along_z, aliases=through)
    swapped = from_core(back)
    links, near = call(near_kernel, [held, field], links, here, along_x, along_z, aliases=through)
    twice, sums = call(
        second_far_kernel,
        [field, struct((128, 1, WIDE))],
        links,
        near,
        swapped,
        source,
        image,
        full,
        rows,
    )
    sums = lax.all_to_all(sums, ("ta", "xyz"), 0, 0)
    return call(last_kernel, [field, field], sums, source, image, full, twice)


def solution(mesh):
    in_specs = (
        P("ta", None, "xyz", None, None, None),
        P("ta", None, "xyz", None, None, None, None),
        P(None, "ta", "xyz", None, None, None),
    )
    out_specs = (P("ta", "xyz", None, None), P("ta", "xyz", None, None))
    return jax.shard_map(
        on_device, mesh=mesh, in_specs=in_specs, out_specs=out_specs, check_vma=False
    )
```

time: 284 us -> 57.6 us (0.20)
  blocking collectives: 129 us -> 28.8 us
  waiting for transfers between devices: 71.8 us -> 3.62 us
  between operations: 19.2 us -> 0.7 us
  local copies, waits for them, and re-layouts: 17.7 us -> 0 us
  matrix products: 15.6 us -> 0 us
  Pallas kernels: 0 us -> 12.8 us
  other arithmetic: 12.8 us -> 0 us
  starting transfers between devices: 16.7 us -> 11.6 us
    psum x2 -> x0, blocking collectives: 129 us -> none  [on_device(): lax.psum((jnp.sum(image_real * residual_real + image_imag * residual_imag...]
    reduce_scatter x1 -> x0, waiting for transfers between devices: 59.9 us -> none  [on_device(): source = lax.psum_scatter(merged, 'ta', scatter_dimension=0, tiled=True)]
    all_to_all x0 -> x2, blocking collectives: none -> 28.8 us  [the longest x1 15.6 us: on_device(): sums = lax.all_to_all(sums, ('ta', 'xyz'), 0, 0)]
    dot_general x3 -> x0, matrix products: 15.6 us -> none  [the longest x1 7.96 us: restrict_local(): jnp.einsum('xzycof,xzyckf->xzyock', rotated(field), vectors, preferred_el...]
    pallas_call x0 -> x12, Pallas kernels: none -> 12.8 us  [call(): pl.pallas_call(kernel, in_specs=specs or [VMEM] * len(args), out_specs=[V...]
    another operation x6 -> x0, local copies, waits for them, and re-layouts: 10.1 us -> none  [the longest x2 9.66 us: rotated(): return jnp.stack([values, turned], axis=-2)]
    ppermute x10 -> x7, waiting for transfers between devices: 12 us -> 3.62 us  [the longest x3 2.23 us: from_core(): lax.ppermute(block, 'ta', [(i, i ^ 1) for i in range(lax.axis_size('ta'))])]
    unnamed x9 -> x0, local copies, waits for them, and re-layouts: 6.87 us -> none
  transfers between devices with their start and end apart: 11 -> 7, of which waited for: 6 -> 4; matrix products, arithmetic and copies ran while one was open for 0% -> 0% of each run, Pallas kernels for 0% -> 8%
where the time goes in v3:
time: 57.6 us; the launch traced here: 57.5 us
  blocking collectives  28.8 us (50%)
  Pallas kernels  12.8 us (22%)
  starting transfers between devices  11.6 us (20%)
  waiting for transfers between devices  3.62 us (6%)
  between operations  0.7 us (1%)
    all_to_all x1, blocking collectives, on_device(): sums = lax.all_to_all(sums, ('ta', 'xyz'), 0, 0)  15.6 us
    all_to_all x1, blocking collectives, on_device(): received = lax.all_to_all(send, 'ta', 0, 0)  13.2 us
    pallas_call x12, Pallas kernels, call(): pl.pallas_call(kernel, in_specs=specs or [VMEM] * len(args), out_specs=[V...  12.8 us
    ppermute x2, starting transfers between devices, z_step(): return lax.ppermute(block, ('ta', 'xyz'), route)  8.51 us
    ppermute x3, waiting for transfers between devices, from_core(): lax.ppermute(block, 'ta', [(i, i ^ 1) for i in range(lax.axis_size('ta'))])  2.23 us
    ppermute x3, starting transfers between devices, from_core(): lax.ppermute(block, 'ta', [(i, i ^ 1) for i in range(lax.axis_size('ta'))])  2.17 us
    ppermute x2, waiting for transfers between devices, x_step(): lax.ppermute(block, 'ta', [(i, (i + (2 if i % 2 == 0 else -2)) % count) f...  1.38 us
  transfers between devices with their start and end apart: 7, of which 4 were waited for; matrix products, arithmetic and copies ran while one was open for 0% of the time, Pallas kernels for 8%

profile of v3, /device:TPU:1, one launch (start us, length us, event | category | flops | bytes accessed | tf_op | source)
XLA Modules:
  0.0 57.5 jit_solution(4212676270620762968)
XLA Ops:
  0.6 6.2 %restrict_kernel.1 = f32[16,2,8,128]{3,2,1,0:T(8,128)S(1)} custom-call(bf16[1,8,2,8,2,768]{5,4,3,2,1,0:T(2,128)(2,1)} %field_hbm.1, bf16[1,8,2,8,2,32,768]{6,5,4,3,2,1,0:T(8,128)(2,1)} %vectors_hbm.1), custom_call_target="tpu_custom_call" | custom-call | tf_op jit(solution)/shard_map/restrict_kernel/pallas_call | solution.py:319
  6.9 13.2 %all_to_all.10.received_ref = f32[16,2,8,128]{3,2,1,0:T(8,128)S(1)} all-to-all(f32[16,2,8,128]{3,2,1,0:T(8,128)S(1)} %restrict_kernel.1), channel_id=1, replica_groups=mesh['ta'=16,'xyz'=8] {'ta'}, dimensions={0} | all-to-all | bytes 262144 | tf_op jit(solution)/shard_map/all_to_all | solution.py:359
  20.1 5.6 %collective-permute-start.1 = (bf16[12,8,128]{2,1,0:T(8,128)(2,1)S(1)}, bf16[12,8,128]{2,1,0:T(8,128)(2,1)S(1)}, u32[]{:S(2)}, u32[]{:S(2)}) collective-permute-start(bf16[12,8,128]{2,1,0:T(8,128)(2,1)S(1)} %get-tuple-element.33), channel_id=1, source_target_pairs={{0,1},{1,2},{2,3},{3,4},{4,5},{5,6},{6,7},{7,0},{8,15},{9,8},{10,9... | collective-permute-start | bytes 73736 | tf_op jit(solution)/shard_map/ppermute | solution.py:310
  25.7 0.5 collective-permute-start
  26.1 2.9 %first_here_kernel.1 = (bf16[9,2,2,8,64,128]{5,4,3,2,1,0:T(8,128)(2,1)S(1)}, f32[2,2,8,128]{3,2,1,0:T(8,128)S(1)}, f32[2,2,8,128]{3,2,1,0:T(8,128)S(1)}) custom-call(bf16[9,2,2,8,64,128]{5,4,3,2,1,0:T(8,128)(2,1)} %links_hbm.1, f32[2,2,8,128]{3,2,1,0:T(8,128)S(1)} %get-tuple-element.29.source_ref, bf16[2,2,8,128]{3,2,1,0:T(8,128)(2,1)S(1)} %get-tuple-element.30.other_ref), custom_call_target="tpu_custom_call" | custom-call | tf_op jit(solution)/shard_map/first_here_kernel/pallas_call | solution.py:319
  29.0 0.0 collective-permute-done.along_x_ref
  29.0 0.0 collective-permute-done.1.along_z_ref
  29.0 0.1 collective-permute-start.2
  29.1 0.4 near_kernel.2
  29.5 0.8 %collective-permute-done.2.swapped_ref = bf16[2,3,8,128]{3,2,1,0:T(8,128)(2,1)S(1)} collective-permute-done((bf16[2,3,8,128]{3,2,1,0:T(8,128)(2,1)S(1)}, bf16[2,3,8,128]{3,2,1,0:T(8,128)(2,1)S(1)}, u32[]{:S(2)}, u32[]{:S(2)}) %collective-permute-start.2) | collective-permute-done | bytes 12320 | tf_op jit(solution)/shard_map/ppermute | solution.py:296
  30.3 0.4 first_far_kernel.1
  30.7 0.2 collective-permute-start.3
  30.9 1.0 %collective-permute-done.3.other_ref = bf16[2,2,8,128]{3,2,1,0:T(8,128)(2,1)S(1)} collective-permute-done((bf16[2,2,8,128]{3,2,1,0:T(8,128)(2,1)S(1)}, bf16[2,2,8,128]{3,2,1,0:T(8,128)(2,1)S(1)}, u32[]{:S(2)}, u32[]{:S(2)}) %collective-permute-start.3) | collective-permute-done | bytes 8224 | tf_op jit(solution)/shard_map/ppermute | solution.py:296
  31.9 2.9 %collective-permute-start.5 = (bf16[12,8,128]{2,1,0:T(8,128)(2,1)S(1)}, bf16[12,8,128]{2,1,0:T(8,128)(2,1)S(1)}, u32[]{:S(2)}, u32[]{:S(2)}) collective-permute-start(bf16[12,8,128]{2,1,0:T(8,128)(2,1)S(1)} %get-tuple-element.47), channel_id=1, source_target_pairs={{0,1},{1,2},{2,3},{3,4},{4,5},{5,6},{6,7},{7,0},{8,15},{9,8},{10,9... | collective-permute-start | bytes 73736 | tf_op jit(solution)/shard_map/ppermute | solution.py:310
  34.9 0.5 collective-permute-start.4
  35.3 1.1 %second_here_kernel.1 = (bf16[9,2,2,8,64,128]{5,4,3,2,1,0:T(8,128)(2,1)S(1)}, f32[2,2,8,128]{3,2,1,0:T(8,128)S(1)}, f32[8,128]{1,0:T(8,128)S(1)}) custom-call(bf16[9,2,2,8,64,128]{5,4,3,2,1,0:T(8,128)(2,1)S(1)} %get-tuple-element.42.links_ref, f32[2,2,8,128]{3,2,1,0:T(8,128)S(1)} %get-tuple-element.43.image_ref, ...), custom_call_target="tpu_custom_call", output_to_operand_aliasing={{0}: (0, {})} | custom-call | tf_op jit(solution)/shard_map/second_here_kernel/pallas_call | solution.py:319
  36.4 1.4 %collective-permute-done.4.along_x_ref = bf16[4,2,8,128]{3,2,1,0:T(8,128)(2,1)S(1)} collective-permute-done((bf16[4,2,8,128]{3,2,1,0:T(8,128)(2,1)S(1)}, bf16[4,2,8,128]{3,2,1,0:T(8,128)(2,1)S(1)}, u32[]{:S(2)}, u32[]{:S(2)}) %collective-permute-start.4) | collective-permute-done | bytes 16416 | tf_op jit(solution)/shard_map/ppermute | solution.py:315
  37.8 0.0 collective-permute-done.5.along_z_ref
  37.8 1.8 %collective-permute-start.6 = (bf16[2,3,8,128]{3,2,1,0:T(8,128)(2,1)S(1)}, bf16[2,3,8,128]{3,2,1,0:T(8,128)(2,1)S(1)}, u32[]{:S(2)}, u32[]{:S(2)}) collective-permute-start(bf16[2,3,8,128]{3,2,1,0:T(8,128)(2,1)S(1)} %get-tuple-element.52), channel_id=1, source_target_pairs={{0,8},{8,0},{16,24},{24,16},{32,40},{40,32},{48,56},{56,48},{64,72... | collective-permute-start | bytes 36872 | tf_op jit(solution)/shard_map/ppermute | solution.py:296
  39.6 0.4 near_kernel.3
  40.0 0.5 collective-permute-done.6.swapped_ref
  40.4 0.6 %second_far_kernel.1 = (f32[2,2,8,128]{3,2,1,0:T(8,128)S(1)}, f32[128,1,128]{2,1,0:T(1,128)S(1)}) custom-call(bf16[9,2,2,8,64,128]{5,4,3,2,1,0:T(8,128)(2,1)S(1)} %get-tuple-element.50.links_ref, f32[2,2,8,128]{3,2,1,0:T(8,128)S(1)} %get-tuple-element.51.near_ref, bf16[2,3,8,128]{3,2,1,0:T(8,128)(2,1)S(1)} %collective-permute-done.6.swapped_ref, ...), custom_call_target="tpu_custom_call" | custom-call | tf_op jit(solution)/shard_map/second_far_kernel/pallas_call | solution.py:319
  41.1 15.6 %all_to_all.11.sums_ref = f32[128,1,128]{2,1,0:T(1,128)S(1)} all-to-all(f32[128,1,128]{2,1,0:T(1,128)S(1)} %get-tuple-element.54), channel_id=1, replica_groups=mesh['ta'=16,'xyz'=8] {'ta','xyz'}, dimensions={0} | all-to-all | bytes 131072 | tf_op jit(solution)/shard_map/all_to_all | solution.py:399
  56.7 0.8 %last_kernel.1 = (f32[2,2,8,128]{3,2,1,0:T(8,128)}, f32[2,2,8,128]{3,2,1,0:T(8,128)}) custom-call(f32[128,1,128]{2,1,0:T(1,128)S(1)} %all_to_all.11.sums_ref, f32[2,2,8,128]{3,2,1,0:T(8,128)S(1)} %get-tuple-element.29.source_ref, f32[2,2,8,128]{3,2,1,0:T(8,128)S(1)} %get-tuple-element.43.image_ref, f32[2,2,8,128]{3,2,1,0:T(8,128)S(1)} %get-tuple-element.44.full_ref, ...), custom_call_target="tpu_custom_call" | custom-call | tf_op jit(solution)/shard_map/last_kernel/pallas_call | solution.py:319
  (4 shorter events, 0.0 us)
Async XLA Ops:
  20.1 8.9 %collective-permute-start.1 = (bf16[12,8,128]{2,1,0:T(8,128)(2,1)S(1)}, bf16[12,8,128]{2,1,0:T(8,128)(2,1)S(1)}, u32[]{:S(2)}, u32[]{:S(2)}) collective-permute-start(bf16[12,8,128]{2,1,0:T(8,128)(2,1)S(1)} %get-tuple-element.33), channel_id=1, source_target_pairs={{0,1},{1,2},{2,3},{3,4},{4,5},{5,6},{6,7},{7,0},{8,15},{9,8},{10,9... | collective-permute-start | bytes 73736 | tf_op jit(solution)/shard_map/ppermute | solution.py:310
  25.7 3.3 %collective-permute-start = (bf16[4,2,8,128]{3,2,1,0:T(8,128)(2,1)S(1)}, bf16[4,2,8,128]{3,2,1,0:T(8,128)(2,1)S(1)}, u32[]{:S(2)}, u32[]{:S(2)}) collective-permute-start(bf16[4,2,8,128]{3,2,1,0:T(8,128)(2,1)S(1)} %get-tuple-element.32), channel_id=1, source_target_pairs={{0,16},{8,120},{16,32},{24,8},{32,48},{40,24},{48,64},{56,40},{64,... | collective-permute-start | bytes 49160 | tf_op jit(solution)/shard_map/ppermute | solution.py:315
  29.0 1.3 %collective-permute-start.2 = (bf16[2,3,8,128]{3,2,1,0:T(8,128)(2,1)S(1)}, bf16[2,3,8,128]{3,2,1,0:T(8,128)(2,1)S(1)}, u32[]{:S(2)}, u32[]{:S(2)}) collective-permute-start(bf16[2,3,8,128]{3,2,1,0:T(8,128)(2,1)S(1)} %get-tuple-element.39), channel_id=1, source_target_pairs={{0,8},{8,0},{16,24},{24,16},{32,40},{40,32},{48,56},{56,48},{64,72... | collective-permute-start | bytes 36872 | tf_op jit(solution)/shard_map/ppermute | solution.py:296
  30.7 1.2 %collective-permute-start.3 = (bf16[2,2,8,128]{3,2,1,0:T(8,128)(2,1)S(1)}, bf16[2,2,8,128]{3,2,1,0:T(8,128)(2,1)S(1)}, u32[]{:S(2)}, u32[]{:S(2)}) collective-permute-start(bf16[2,2,8,128]{3,2,1,0:T(8,128)(2,1)S(1)} %get-tuple-element.41.own_ref), channel_id=1, source_target_pairs={{0,8},{8,0},{16,24},{24,16},{32,40},{40,32},{48,56},{56,48},{64,72... | collective-permute-start | bytes 24584 | tf_op jit(solution)/shard_map/ppermute | solution.py:296
  31.9 5.8 %collective-permute-start.5 = (bf16[12,8,128]{2,1,0:T(8,128)(2,1)S(1)}, bf16[12,8,128]{2,1,0:T(8,128)(2,1)S(1)}, u32[]{:S(2)}, u32[]{:S(2)}) collective-permute-start(bf16[12,8,128]{2,1,0:T(8,128)(2,1)S(1)} %get-tuple-element.47), channel_id=1, source_target_pairs={{0,1},{1,2},{2,3},{3,4},{4,5},{5,6},{6,7},{7,0},{8,15},{9,8},{10,9... | collective-permute-start | bytes 73736 | tf_op jit(solution)/shard_map/ppermute | solution.py:310
  34.9 2.9 %collective-permute-start.4 = (bf16[4,2,8,128]{3,2,1,0:T(8,128)(2,1)S(1)}, bf16[4,2,8,128]{3,2,1,0:T(8,128)(2,1)S(1)}, u32[]{:S(2)}, u32[]{:S(2)}) collective-permute-start(bf16[4,2,8,128]{3,2,1,0:T(8,128)(2,1)S(1)} %get-tuple-element.46), channel_id=1, source_target_pairs={{0,16},{8,120},{16,32},{24,8},{32,48},{40,24},{48,64},{56,40},{64,... | collective-permute-start | bytes 49160 | tf_op jit(solution)/shard_map/ppermute | solution.py:315
  37.8 2.7 %collective-permute-start.6 = (bf16[2,3,8,128]{3,2,1,0:T(8,128)(2,1)S(1)}, bf16[2,3,8,128]{3,2,1,0:T(8,128)(2,1)S(1)}, u32[]{:S(2)}, u32[]{:S(2)}) collective-permute-start(bf16[2,3,8,128]{3,2,1,0:T(8,128)(2,1)S(1)} %get-tuple-element.52), channel_id=1, source_target_pairs={{0,8},{8,0},{16,24},{24,16},{32,40},{40,32},{48,56},{56,48},{64,72... | collective-permute-start | bytes 36872 | tf_op jit(solution)/shard_map/ppermute | solution.py:296

commit v4 on v3

--- a/solution.py
+++ b/solution.py
@@ -83,8 +83,7 @@
 
 
 def edge_of(chip):
-    plane = jnp.where(lax.axis_index("ta") % 2 == 1, chip[:, 0], chip[:, 1])
-    return jnp.concatenate([plane, jnp.zeros((EDGE - 4,) + plane.shape[1:], F32)], axis=0).astype(BF16)
+    return jnp.where(lax.axis_index("ta") % 2 == 1, chip[:, 0], chip[:, 1]).astype(BF16)
 
 
 def gather_kernel(received_ref, source_ref, other_ref, chip_ref, edge_ref):
@@ -211,7 +210,8 @@
 def chip_kernel(_, own_ref, other_ref, links_ref, chip_ref, edge_ref):
     chip_ref[:2] = own_ref[...]
     chip_ref[2:] = other_ref[...]
-    edge_ref[...] = edge_of(chip_ref[...].astype(F32))
+    edge_ref[:4] = edge_of(chip_ref[...].astype(F32))
+    edge_ref[4:] = jnp.zeros((EDGE - 4, 8, WIDE), BF16)
 
 
 def swap_kernel(_, along_x_ref, along_z_ref, links_ref, back_ref):
@@ -336,7 +336,7 @@
     hbm = pl.BlockSpec(memory_space=pltpu.HBM)
     site = (2, 2, 8, WIDE)
     field, coarse = struct(site), struct(site, BF16)
-    chip_rows, edge_rows = struct((4, 2, 8, WIDE), BF16), struct((EDGE, 8, WIDE), BF16)
+    chip_rows, edge_rows = struct((4, 2, 8, WIDE), BF16), struct((4, 8, WIDE), BF16)
     back_rows = struct((2, 3, 8, WIDE), BF16)
     held = pltpu.VMEM(coarse_links.shape, BF16)
     through = ((0, 0),)
@@ -377,7 +377,7 @@
     )
 
     other = from_core(own)
-    links, chip, edge = call(chip_kernel, [held, chip_rows, edge_rows], links, own, other, aliases=through)
+    links, chip, edge = call(chip_kernel, [held, chip_rows, struct((EDGE, 8, WIDE), BF16)], links, own, other, aliases=through)
     along_x, along_z = x_step(chip), z_step(edge)
     links, here, rows = call(
         second_here_kernel, [held, field, struct((8, WIDE))], links, image, other, source, full, aliases=through

time: 57.6 us -> 57.3 us (level)
  blocking collectives: 28.8 us -> 27.9 us
    all_to_all x1, blocking collectives: 15.6 us -> 14.7 us  [on_device(): sums = lax.all_to_all(sums, ('ta', 'xyz'), 0, 0)]
where the time goes in v4:
time: 57.3 us; the launch traced here: 57.2 us
  blocking collectives  27.9 us (49%)
  Pallas kernels  12.8 us (22%)
  starting transfers between devices  11.7 us (20%)
  waiting for transfers between devices  4.06 us (7%)
  between operations  0.7 us (1%)
    all_to_all x1, blocking collectives, on_device(): sums = lax.all_to_all(sums, ('ta', 'xyz'), 0, 0)  14.7 us
    all_to_all x1, blocking collectives, on_device(): received = lax.all_to_all(send, 'ta', 0, 0)  13.2 us
    pallas_call x12, Pallas kernels, call(): pl.pallas_call(kernel, in_specs=specs or [VMEM] * len(args), out_specs=[V...  12.8 us
    ppermute x2, starting transfers between devices, z_step(): return lax.ppermute(block, ('ta', 'xyz'), route)  8.72 us
    ppermute x3, waiting for transfers between devices, from_core(): lax.ppermute(block, 'ta', [(i, i ^ 1) for i in range(lax.axis_size('ta'))])  2.23 us
    ppermute x3, starting transfers between devices, from_core(): lax.ppermute(block, 'ta', [(i, i ^ 1) for i in range(lax.axis_size('ta'))])  1.89 us
    ppermute x2, waiting for transfers between devices, x_step(): lax.ppermute(block, 'ta', [(i, (i + (2 if i % 2 == 0 else -2)) % count) f...  1.83 us
  transfers between devices with their start and end apart: 7, of which 4 were waited for; matrix products, arithmetic and copies ran while one was open for 0% of the time, Pallas kernels for 8%

profile of v4, /device:TPU:1, one launch (start us, length us, event | category | flops | bytes accessed | tf_op | source)
XLA Modules:
  0.0 57.2 jit_solution(5002058886727069941)
XLA Ops:
  0.6 6.2 %restrict_kernel.1 = f32[16,2,8,128]{3,2,1,0:T(8,128)S(1)} custom-call(bf16[1,8,2,8,2,768]{5,4,3,2,1,0:T(2,128)(2,1)} %field_hbm.1, bf16[1,8,2,8,2,32,768]{6,5,4,3,2,1,0:T(8,128)(2,1)} %vectors_hbm.1), custom_call_target="tpu_custom_call" | custom-call | tf_op jit(solution)/shard_map/restrict_kernel/pallas_call | solution.py:319
  6.9 13.2 %all_to_all.10.received_ref = f32[16,2,8,128]{3,2,1,0:T(8,128)S(1)} all-to-all(f32[16,2,8,128]{3,2,1,0:T(8,128)S(1)} %restrict_kernel.1), channel_id=1, replica_groups=mesh['ta'=16,'xyz'=8] {'ta'}, dimensions={0} | all-to-all | bytes 262144 | tf_op jit(solution)/shard_map/all_to_all | solution.py:359
  20.1 1.1 %collective-permute-start = (bf16[4,2,8,128]{3,2,1,0:T(8,128)(2,1)S(1)}, bf16[4,2,8,128]{3,2,1,0:T(8,128)(2,1)S(1)}, u32[]{:S(2)}, u32[]{:S(2)}) collective-permute-start(bf16[4,2,8,128]{3,2,1,0:T(8,128)(2,1)S(1)} %get-tuple-element.32), channel_id=1, source_target_pairs={{0,16},{8,120},{16,32},{24,8},{32,48},{40,24},{48,64},{56,40},{64,... | collective-permute-start | bytes 49160 | tf_op jit(solution)/shard_map/ppermute | solution.py:315
  21.2 5.5 %collective-permute-start.1 = (bf16[4,8,128]{2,1,0:T(8,128)(2,1)S(1)}, bf16[4,8,128]{2,1,0:T(8,128)(2,1)S(1)}, u32[]{:S(2)}, u32[]{:S(2)}) collective-permute-start(bf16[4,8,128]{2,1,0:T(8,128)(2,1)S(1)} %get-tuple-element.33), channel_id=1, source_target_pairs={{0,1},{1,2},{2,3},{3,4},{4,5},{5,6},{6,7},{7,0},{8,15},{9,8},{10,9... | collective-permute-start | bytes 24584 | tf_op jit(solution)/shard_map/ppermute | solution.py:310
  26.7 2.9 %first_here_kernel.1 = (bf16[9,2,2,8,64,128]{5,4,3,2,1,0:T(8,128)(2,1)S(1)}, f32[2,2,8,128]{3,2,1,0:T(8,128)S(1)}, f32[2,2,8,128]{3,2,1,0:T(8,128)S(1)}) custom-call(bf16[9,2,2,8,64,128]{5,4,3,2,1,0:T(8,128)(2,1)} %links_hbm.1, f32[2,2,8,128]{3,2,1,0:T(8,128)S(1)} %get-tuple-element.29.source_ref, bf16[2,2,8,128]{3,2,1,0:T(8,128)(2,1)S(1)} %get-tuple-element.30.other_ref), custom_call_target="tpu_custom_call" | custom-call | tf_op jit(solution)/shard_map/first_here_kernel/pallas_call | solution.py:319
  29.6 0.0 collective-permute-done.1.along_z_ref
  29.6 0.0 collective-permute-done.along_x_ref
  29.6 0.1 collective-permute-start.2
  29.7 0.4 near_kernel.2
  30.1 0.8 %collective-permute-done.2.swapped_ref = bf16[2,3,8,128]{3,2,1,0:T(8,128)(2,1)S(1)} collective-permute-done((bf16[2,3,8,128]{3,2,1,0:T(8,128)(2,1)S(1)}, bf16[2,3,8,128]{3,2,1,0:T(8,128)(2,1)S(1)}, u32[]{:S(2)}, u32[]{:S(2)}) %collective-permute-start.2) | collective-permute-done | bytes 12320 | tf_op jit(solution)/shard_map/ppermute | solution.py:296
  30.9 0.4 first_far_kernel.1
  31.3 0.2 collective-permute-start.3
  31.5 1.0 %collective-permute-done.3.other_ref = bf16[2,2,8,128]{3,2,1,0:T(8,128)(2,1)S(1)} collective-permute-done((bf16[2,2,8,128]{3,2,1,0:T(8,128)(2,1)S(1)}, bf16[2,2,8,128]{3,2,1,0:T(8,128)(2,1)S(1)}, u32[]{:S(2)}, u32[]{:S(2)}) %collective-permute-start.3) | collective-permute-done | bytes 8224 | tf_op jit(solution)/shard_map/ppermute | solution.py:296
  32.5 3.2 %collective-permute-start.5 = (bf16[12,8,128]{2,1,0:T(8,128)(2,1)S(1)}, bf16[12,8,128]{2,1,0:T(8,128)(2,1)S(1)}, u32[]{:S(2)}, u32[]{:S(2)}) collective-permute-start(bf16[12,8,128]{2,1,0:T(8,128)(2,1)S(1)} %get-tuple-element.47), channel_id=1, source_target_pairs={{0,1},{1,2},{2,3},{3,4},{4,5},{5,6},{6,7},{7,0},{8,15},{9,8},{10,9... | collective-permute-start | bytes 73736 | tf_op jit(solution)/shard_map/ppermute | solution.py:310
  35.8 0.0 collective-permute-start.4
  35.8 1.1 %second_here_kernel.1 = (bf16[9,2,2,8,64,128]{5,4,3,2,1,0:T(8,128)(2,1)S(1)}, f32[2,2,8,128]{3,2,1,0:T(8,128)S(1)}, f32[8,128]{1,0:T(8,128)S(1)}) custom-call(bf16[9,2,2,8,64,128]{5,4,3,2,1,0:T(8,128)(2,1)S(1)} %get-tuple-element.42.links_ref, f32[2,2,8,128]{3,2,1,0:T(8,128)S(1)} %get-tuple-element.43.image_ref, ...), custom_call_target="tpu_custom_call", output_to_operand_aliasing={{0}: (0, {})} | custom-call | tf_op jit(solution)/shard_map/second_here_kernel/pallas_call | solution.py:319
  36.8 1.8 %collective-permute-done.4.along_x_ref = bf16[4,2,8,128]{3,2,1,0:T(8,128)(2,1)S(1)} collective-permute-done((bf16[4,2,8,128]{3,2,1,0:T(8,128)(2,1)S(1)}, bf16[4,2,8,128]{3,2,1,0:T(8,128)(2,1)S(1)}, u32[]{:S(2)}, u32[]{:S(2)}) %collective-permute-start.4) | collective-permute-done | bytes 16416 | tf_op jit(solution)/shard_map/ppermute | solution.py:315
  38.6 0.0 collective-permute-done.5.along_z_ref
  38.7 1.6 %collective-permute-start.6 = (bf16[2,3,8,128]{3,2,1,0:T(8,128)(2,1)S(1)}, bf16[2,3,8,128]{3,2,1,0:T(8,128)(2,1)S(1)}, u32[]{:S(2)}, u32[]{:S(2)}) collective-permute-start(bf16[2,3,8,128]{3,2,1,0:T(8,128)(2,1)S(1)} %get-tuple-element.52), channel_id=1, source_target_pairs={{0,8},{8,0},{16,24},{24,16},{32,40},{40,32},{48,56},{56,48},{64,72... | collective-permute-start | bytes 36872 | tf_op jit(solution)/shard_map/ppermute | solution.py:296
  40.2 0.4 near_kernel.3
  40.6 0.5 collective-permute-done.6.swapped_ref
  41.1 0.6 %second_far_kernel.1 = (f32[2,2,8,128]{3,2,1,0:T(8,128)S(1)}, f32[128,1,128]{2,1,0:T(1,128)S(1)}) custom-call(bf16[9,2,2,8,64,128]{5,4,3,2,1,0:T(8,128)(2,1)S(1)} %get-tuple-element.50.links_ref, f32[2,2,8,128]{3,2,1,0:T(8,128)S(1)} %get-tuple-element.51.near_ref, bf16[2,3,8,128]{3,2,1,0:T(8,128)(2,1)S(1)} %collective-permute-done.6.swapped_ref, ...), custom_call_target="tpu_custom_call" | custom-call | tf_op jit(solution)/shard_map/second_far_kernel/pallas_call | solution.py:319
  41.7 14.7 %all_to_all.11.sums_ref = f32[128,1,128]{2,1,0:T(1,128)S(1)} all-to-all(f32[128,1,128]{2,1,0:T(1,128)S(1)} %get-tuple-element.54), channel_id=1, replica_groups=mesh['ta'=16,'xyz'=8] {'ta','xyz'}, dimensions={0} | all-to-all | bytes 131072 | tf_op jit(solution)/shard_map/all_to_all | solution.py:399
  56.4 0.8 %last_kernel.1 = (f32[2,2,8,128]{3,2,1,0:T(8,128)}, f32[2,2,8,128]{3,2,1,0:T(8,128)}) custom-call(f32[128,1,128]{2,1,0:T(1,128)S(1)} %all_to_all.11.sums_ref, f32[2,2,8,128]{3,2,1,0:T(8,128)S(1)} %get-tuple-element.29.source_ref, f32[2,2,8,128]{3,2,1,0:T(8,128)S(1)} %get-tuple-element.43.image_ref, f32[2,2,8,128]{3,2,1,0:T(8,128)S(1)} %get-tuple-element.44.full_ref, ...), custom_call_target="tpu_custom_call" | custom-call | tf_op jit(solution)/shard_map/last_kernel/pallas_call | solution.py:319
  (4 shorter events, 0.0 us)
Async XLA Ops:
  20.1 9.5 %collective-permute-start = (bf16[4,2,8,128]{3,2,1,0:T(8,128)(2,1)S(1)}, bf16[4,2,8,128]{3,2,1,0:T(8,128)(2,1)S(1)}, u32[]{:S(2)}, u32[]{:S(2)}) collective-permute-start(bf16[4,2,8,128]{3,2,1,0:T(8,128)(2,1)S(1)} %get-tuple-element.32), channel_id=1, source_target_pairs={{0,16},{8,120},{16,32},{24,8},{32,48},{40,24},{48,64},{56,40},{64,... | collective-permute-start | bytes 49160 | tf_op jit(solution)/shard_map/ppermute | solution.py:315
  21.2 8.4 %collective-permute-start.1 = (bf16[4,8,128]{2,1,0:T(8,128)(2,1)S(1)}, bf16[4,8,128]{2,1,0:T(8,128)(2,1)S(1)}, u32[]{:S(2)}, u32[]{:S(2)}) collective-permute-start(bf16[4,8,128]{2,1,0:T(8,128)(2,1)S(1)} %get-tuple-element.33), channel_id=1, source_target_pairs={{0,1},{1,2},{2,3},{3,4},{4,5},{5,6},{6,7},{7,0},{8,15},{9,8},{10,9... | collective-permute-start | bytes 24584 | tf_op jit(solution)/shard_map/ppermute | solution.py:310
  29.6 1.3 %collective-permute-start.2 = (bf16[2,3,8,128]{3,2,1,0:T(8,128)(2,1)S(1)}, bf16[2,3,8,128]{3,2,1,0:T(8,128)(2,1)S(1)}, u32[]{:S(2)}, u32[]{:S(2)}) collective-permute-start(bf16[2,3,8,128]{3,2,1,0:T(8,128)(2,1)S(1)} %get-tuple-element.39), channel_id=1, source_target_pairs={{0,8},{8,0},{16,24},{24,16},{32,40},{40,32},{48,56},{56,48},{64,72... | collective-permute-start | bytes 36872 | tf_op jit(solution)/shard_map/ppermute | solution.py:296
  31.3 1.2 %collective-permute-start.3 = (bf16[2,2,8,128]{3,2,1,0:T(8,128)(2,1)S(1)}, bf16[2,2,8,128]{3,2,1,0:T(8,128)(2,1)S(1)}, u32[]{:S(2)}, u32[]{:S(2)}) collective-permute-start(bf16[2,2,8,128]{3,2,1,0:T(8,128)(2,1)S(1)} %get-tuple-element.41.own_ref), channel_id=1, source_target_pairs={{0,8},{8,0},{16,24},{24,16},{32,40},{40,32},{48,56},{56,48},{64,72... | collective-permute-start | bytes 24584 | tf_op jit(solution)/shard_map/ppermute | solution.py:296
  32.5 6.1 %collective-permute-start.5 = (bf16[12,8,128]{2,1,0:T(8,128)(2,1)S(1)}, bf16[12,8,128]{2,1,0:T(8,128)(2,1)S(1)}, u32[]{:S(2)}, u32[]{:S(2)}) collective-permute-start(bf16[12,8,128]{2,1,0:T(8,128)(2,1)S(1)} %get-tuple-element.47), channel_id=1, source_target_pairs={{0,1},{1,2},{2,3},{3,4},{4,5},{5,6},{6,7},{7,0},{8,15},{9,8},{10,9... | collective-permute-start | bytes 73736 | tf_op jit(solution)/shard_map/ppermute | solution.py:310
  35.8 2.9 %collective-permute-start.4 = (bf16[4,2,8,128]{3,2,1,0:T(8,128)(2,1)S(1)}, bf16[4,2,8,128]{3,2,1,0:T(8,128)(2,1)S(1)}, u32[]{:S(2)}, u32[]{:S(2)}) collective-permute-start(bf16[4,2,8,128]{3,2,1,0:T(8,128)(2,1)S(1)} %get-tuple-element.46), channel_id=1, source_target_pairs={{0,16},{8,120},{16,32},{24,8},{32,48},{40,24},{48,64},{56,40},{64,... | collective-permute-start | bytes 49160 | tf_op jit(solution)/shard_map/ppermute | solution.py:315
  38.7 2.4 %collective-permute-start.6 = (bf16[2,3,8,128]{3,2,1,0:T(8,128)(2,1)S(1)}, bf16[2,3,8,128]{3,2,1,0:T(8,128)(2,1)S(1)}, u32[]{:S(2)}, u32[]{:S(2)}) collective-permute-start(bf16[2,3,8,128]{3,2,1,0:T(8,128)(2,1)S(1)} %get-tuple-element.52), channel_id=1, source_target_pairs={{0,8},{8,0},{16,24},{24,16},{32,40},{40,32},{48,56},{56,48},{64,72... | collective-permute-start | bytes 36872 | tf_op jit(solution)/shard_map/ppermute | solution.py:296

commit v5 on v4

--- a/solution.py
+++ b/solution.py
@@ -157,25 +157,23 @@
 
 
 def first_here_kernel(links_hbm, source_ref, other_ref, links_ref, plain_ref, lower_ref, links_sem):
+    parts = (pl.ds(0, 1), pl.ds(3, 6), pl.ds(1, 2))
     copies = [
-        [pltpu.make_async_copy(links_hbm.at[d, r], links_ref.at[d, r], links_sem.at[d, r]) for d in range(9)]
+        [
+            pltpu.make_async_copy(links_hbm.at[part, r], links_ref.at[part, r], links_sem.at[i, r])
+            for i, part in enumerate(parts)
+        ]
         for r in range(2)
     ]
-    here = (0, 3, 4, 5, 6, 7, 8)
-    for r in range(2):
-        for d in here:
-            copies[r][d].start()
-    for r in range(2):
-        for d in (1, 2):
-            copies[r][d].start()
+    for r, i in ((0, 0), (0, 1), (1, 0), (1, 1), (0, 2), (1, 2)):
+        copies[r][i].start()
     source, other = source_ref[...], other_ref[...].astype(F32)
     for r in range(2):
-        for d in here:
-            copies[r][d].wait()
+        copies[r][0].wait()
+        copies[r][1].wait()
         plain_ref[r], lower_ref[r] = applied_here(links_ref, source, other, r)
-    for r in range(2):
-        for d in (1, 2):
-            copies[r][d].wait()
+    copies[0][2].wait()
+    copies[1][2].wait()
 
 
 def near_kernel(links_ref, here_ref, along_x_ref, along_z_ref, _, near_ref):
@@ -367,7 +365,7 @@
         source,
         other,
         specs=[hbm, VMEM, VMEM],
-        scratch=[pltpu.SemaphoreType.DMA((9, 2))],
+        scratch=[pltpu.SemaphoreType.DMA((3, 2))],
     )
     links, back = call(swap_kernel, [held, back_rows], links, along_x, along_z, aliases=through)
     swapped = from_core(back)

time: 57.3 us -> 57.3 us (level)
  no operation moved by 1% of the time
where the time goes in v5:
time: 57.3 us; the launch traced here: 57.2 us
  blocking collectives  27.9 us (49%)
  Pallas kernels  12.7 us (22%)
  starting transfers between devices  11.7 us (20%)
  waiting for transfers between devices  4.06 us (7%)
  between operations  0.7 us (1%)
    all_to_all x1, blocking collectives, on_device(): sums = lax.all_to_all(sums, ('ta', 'xyz'), 0, 0)  14.7 us
    all_to_all x1, blocking collectives, on_device(): received = lax.all_to_all(send, 'ta', 0, 0)  13.2 us
    pallas_call x12, Pallas kernels, call(): pl.pallas_call(kernel, in_specs=specs or [VMEM] * len(args), out_specs=[V...  12.7 us
    ppermute x2, starting transfers between devices, z_step(): return lax.ppermute(block, ('ta', 'xyz'), route)  8.75 us
    ppermute x3, waiting for transfers between devices, from_core(): lax.ppermute(block, 'ta', [(i, i ^ 1) for i in range(lax.axis_size('ta'))])  2.23 us
    ppermute x3, starting transfers between devices, from_core(): lax.ppermute(block, 'ta', [(i, i ^ 1) for i in range(lax.axis_size('ta'))])  1.85 us
    ppermute x2, waiting for transfers between devices, x_step(): lax.ppermute(block, 'ta', [(i, (i + (2 if i % 2 == 0 else -2)) % count) f...  1.83 us
  transfers between devices with their start and end apart: 7, of which 4 were waited for; matrix products, arithmetic and copies ran while one was open for 0% of the time, Pallas kernels for 8%

profile of v5, /device:TPU:1, one launch (start us, length us, event | category | flops | bytes accessed | tf_op | source)
XLA Modules:
  0.0 57.2 jit_solution(17066805455001457565)
XLA Ops:
  0.6 6.2 %restrict_kernel.1 = f32[16,2,8,128]{3,2,1,0:T(8,128)S(1)} custom-call(bf16[1,8,2,8,2,768]{5,4,3,2,1,0:T(2,128)(2,1)} %field_hbm.1, bf16[1,8,2,8,2,32,768]{6,5,4,3,2,1,0:T(8,128)(2,1)} %vectors_hbm.1), custom_call_target="tpu_custom_call" | custom-call | tf_op jit(solution)/shard_map/restrict_kernel/pallas_call | solution.py:317
  6.9 13.2 %all_to_all.10.received_ref = f32[16,2,8,128]{3,2,1,0:T(8,128)S(1)} all-to-all(f32[16,2,8,128]{3,2,1,0:T(8,128)S(1)} %restrict_kernel.1), channel_id=1, replica_groups=mesh['ta'=16,'xyz'=8] {'ta'}, dimensions={0} | all-to-all | bytes 262144 | tf_op jit(solution)/shard_map/all_to_all | solution.py:357
  20.1 1.1 %collective-permute-start = (bf16[4,2,8,128]{3,2,1,0:T(8,128)(2,1)S(1)}, bf16[4,2,8,128]{3,2,1,0:T(8,128)(2,1)S(1)}, u32[]{:S(2)}, u32[]{:S(2)}) collective-permute-start(bf16[4,2,8,128]{3,2,1,0:T(8,128)(2,1)S(1)} %get-tuple-element.32), channel_id=1, source_target_pairs={{0,16},{8,120},{16,32},{24,8},{32,48},{40,24},{48,64},{56,40},{64,... | collective-permute-start | bytes 49160 | tf_op jit(solution)/shard_map/ppermute | solution.py:313
  21.2 5.5 %collective-permute-start.1 = (bf16[4,8,128]{2,1,0:T(8,128)(2,1)S(1)}, bf16[4,8,128]{2,1,0:T(8,128)(2,1)S(1)}, u32[]{:S(2)}, u32[]{:S(2)}) collective-permute-start(bf16[4,8,128]{2,1,0:T(8,128)(2,1)S(1)} %get-tuple-element.33), channel_id=1, source_target_pairs={{0,1},{1,2},{2,3},{3,4},{4,5},{5,6},{6,7},{7,0},{8,15},{9,8},{10,9... | collective-permute-start | bytes 24584 | tf_op jit(solution)/shard_map/ppermute | solution.py:308
  26.7 2.8 %first_here_kernel.1 = (bf16[9,2,2,8,64,128]{5,4,3,2,1,0:T(8,128)(2,1)S(1)}, f32[2,2,8,128]{3,2,1,0:T(8,128)S(1)}, f32[2,2,8,128]{3,2,1,0:T(8,128)S(1)}) custom-call(bf16[9,2,2,8,64,128]{5,4,3,2,1,0:T(8,128)(2,1)} %links_hbm.1, f32[2,2,8,128]{3,2,1,0:T(8,128)S(1)} %get-tuple-element.29.source_ref, bf16[2,2,8,128]{3,2,1,0:T(8,128)(2,1)S(1)} %get-tuple-element.30.other_ref), custom_call_target="tpu_custom_call" | custom-call | tf_op jit(solution)/shard_map/first_here_kernel/pallas_call | solution.py:317
  29.6 0.0 collective-permute-done.1.along_z_ref
  29.6 0.0 collective-permute-done.along_x_ref
  29.6 0.1 collective-permute-start.2
  29.7 0.4 near_kernel.2
  30.1 0.8 %collective-permute-done.2.swapped_ref = bf16[2,3,8,128]{3,2,1,0:T(8,128)(2,1)S(1)} collective-permute-done((bf16[2,3,8,128]{3,2,1,0:T(8,128)(2,1)S(1)}, bf16[2,3,8,128]{3,2,1,0:T(8,128)(2,1)S(1)}, u32[]{:S(2)}, u32[]{:S(2)}) %collective-permute-start.2) | collective-permute-done | bytes 12320 | tf_op jit(solution)/shard_map/ppermute | solution.py:294
  30.9 0.4 first_far_kernel.1
  31.3 0.2 collective-permute-start.3
  31.5 1.0 %collective-permute-done.3.other_ref = bf16[2,2,8,128]{3,2,1,0:T(8,128)(2,1)S(1)} collective-permute-done((bf16[2,2,8,128]{3,2,1,0:T(8,128)(2,1)S(1)}, bf16[2,2,8,128]{3,2,1,0:T(8,128)(2,1)S(1)}, u32[]{:S(2)}, u32[]{:S(2)}) %collective-permute-start.3) | collective-permute-done | bytes 8224 | tf_op jit(solution)/shard_map/ppermute | solution.py:294
  32.5 3.3 %collective-permute-start.5 = (bf16[12,8,128]{2,1,0:T(8,128)(2,1)S(1)}, bf16[12,8,128]{2,1,0:T(8,128)(2,1)S(1)}, u32[]{:S(2)}, u32[]{:S(2)}) collective-permute-start(bf16[12,8,128]{2,1,0:T(8,128)(2,1)S(1)} %get-tuple-element.47), channel_id=1, source_target_pairs={{0,1},{1,2},{2,3},{3,4},{4,5},{5,6},{6,7},{7,0},{8,15},{9,8},{10,9... | collective-permute-start | bytes 73736 | tf_op jit(solution)/shard_map/ppermute | solution.py:308
  35.8 0.0 collective-permute-start.4
  35.8 1.1 %second_here_kernel.1 = (bf16[9,2,2,8,64,128]{5,4,3,2,1,0:T(8,128)(2,1)S(1)}, f32[2,2,8,128]{3,2,1,0:T(8,128)S(1)}, f32[8,128]{1,0:T(8,128)S(1)}) custom-call(bf16[9,2,2,8,64,128]{5,4,3,2,1,0:T(8,128)(2,1)S(1)} %get-tuple-element.42.links_ref, f32[2,2,8,128]{3,2,1,0:T(8,128)S(1)} %get-tuple-element.43.image_ref, ...), custom_call_target="tpu_custom_call", output_to_operand_aliasing={{0}: (0, {})} | custom-call | tf_op jit(solution)/shard_map/second_here_kernel/pallas_call | solution.py:317
  36.8 1.8 %collective-permute-done.4.along_x_ref = bf16[4,2,8,128]{3,2,1,0:T(8,128)(2,1)S(1)} collective-permute-done((bf16[4,2,8,128]{3,2,1,0:T(8,128)(2,1)S(1)}, bf16[4,2,8,128]{3,2,1,0:T(8,128)(2,1)S(1)}, u32[]{:S(2)}, u32[]{:S(2)}) %collective-permute-start.4) | collective-permute-done | bytes 16416 | tf_op jit(solution)/shard_map/ppermute | solution.py:313
  38.6 0.0 collective-permute-done.5.along_z_ref
  38.7 1.5 %collective-permute-start.6 = (bf16[2,3,8,128]{3,2,1,0:T(8,128)(2,1)S(1)}, bf16[2,3,8,128]{3,2,1,0:T(8,128)(2,1)S(1)}, u32[]{:S(2)}, u32[]{:S(2)}) collective-permute-start(bf16[2,3,8,128]{3,2,1,0:T(8,128)(2,1)S(1)} %get-tuple-element.52), channel_id=1, source_target_pairs={{0,8},{8,0},{16,24},{24,16},{32,40},{40,32},{48,56},{56,48},{64,72... | collective-permute-start | bytes 36872 | tf_op jit(solution)/shard_map/ppermute | solution.py:294
  40.2 0.4 near_kernel.3
  40.6 0.5 collective-permute-done.6.swapped_ref
  41.0 0.6 %second_far_kernel.1 = (f32[2,2,8,128]{3,2,1,0:T(8,128)S(1)}, f32[128,1,128]{2,1,0:T(1,128)S(1)}) custom-call(bf16[9,2,2,8,64,128]{5,4,3,2,1,0:T(8,128)(2,1)S(1)} %get-tuple-element.50.links_ref, f32[2,2,8,128]{3,2,1,0:T(8,128)S(1)} %get-tuple-element.51.near_ref, bf16[2,3,8,128]{3,2,1,0:T(8,128)(2,1)S(1)} %collective-permute-done.6.swapped_ref, ...), custom_call_target="tpu_custom_call" | custom-call | tf_op jit(solution)/shard_map/second_far_kernel/pallas_call | solution.py:317
  41.6 14.7 %all_to_all.11.sums_ref = f32[128,1,128]{2,1,0:T(1,128)S(1)} all-to-all(f32[128,1,128]{2,1,0:T(1,128)S(1)} %get-tuple-element.54), channel_id=1, replica_groups=mesh['ta'=16,'xyz'=8] {'ta','xyz'}, dimensions={0} | all-to-all | bytes 131072 | tf_op jit(solution)/shard_map/all_to_all | solution.py:397
  56.4 0.8 %last_kernel.1 = (f32[2,2,8,128]{3,2,1,0:T(8,128)}, f32[2,2,8,128]{3,2,1,0:T(8,128)}) custom-call(f32[128,1,128]{2,1,0:T(1,128)S(1)} %all_to_all.11.sums_ref, f32[2,2,8,128]{3,2,1,0:T(8,128)S(1)} %get-tuple-element.29.source_ref, f32[2,2,8,128]{3,2,1,0:T(8,128)S(1)} %get-tuple-element.43.image_ref, f32[2,2,8,128]{3,2,1,0:T(8,128)S(1)} %get-tuple-element.44.full_ref, ...), custom_call_target="tpu_custom_call" | custom-call | tf_op jit(solution)/shard_map/last_kernel/pallas_call | solution.py:317
  (4 shorter events, 0.0 us)
Async XLA Ops:
  20.1 9.5 %collective-permute-start = (bf16[4,2,8,128]{3,2,1,0:T(8,128)(2,1)S(1)}, bf16[4,2,8,128]{3,2,1,0:T(8,128)(2,1)S(1)}, u32[]{:S(2)}, u32[]{:S(2)}) collective-permute-start(bf16[4,2,8,128]{3,2,1,0:T(8,128)(2,1)S(1)} %get-tuple-element.32), channel_id=1, source_target_pairs={{0,16},{8,120},{16,32},{24,8},{32,48},{40,24},{48,64},{56,40},{64,... | collective-permute-start | bytes 49160 | tf_op jit(solution)/shard_map/ppermute | solution.py:313
  21.2 8.3 %collective-permute-start.1 = (bf16[4,8,128]{2,1,0:T(8,128)(2,1)S(1)}, bf16[4,8,128]{2,1,0:T(8,128)(2,1)S(1)}, u32[]{:S(2)}, u32[]{:S(2)}) collective-permute-start(bf16[4,8,128]{2,1,0:T(8,128)(2,1)S(1)} %get-tuple-element.33), channel_id=1, source_target_pairs={{0,1},{1,2},{2,3},{3,4},{4,5},{5,6},{6,7},{7,0},{8,15},{9,8},{10,9... | collective-permute-start | bytes 24584 | tf_op jit(solution)/shard_map/ppermute | solution.py:308
  29.6 1.3 %collective-permute-start.2 = (bf16[2,3,8,128]{3,2,1,0:T(8,128)(2,1)S(1)}, bf16[2,3,8,128]{3,2,1,0:T(8,128)(2,1)S(1)}, u32[]{:S(2)}, u32[]{:S(2)}) collective-permute-start(bf16[2,3,8,128]{3,2,1,0:T(8,128)(2,1)S(1)} %get-tuple-element.39), channel_id=1, source_target_pairs={{0,8},{8,0},{16,24},{24,16},{32,40},{40,32},{48,56},{56,48},{64,72... | collective-permute-start | bytes 36872 | tf_op jit(solution)/shard_map/ppermute | solution.py:294
  31.3 1.2 %collective-permute-start.3 = (bf16[2,2,8,128]{3,2,1,0:T(8,128)(2,1)S(1)}, bf16[2,2,8,128]{3,2,1,0:T(8,128)(2,1)S(1)}, u32[]{:S(2)}, u32[]{:S(2)}) collective-permute-start(bf16[2,2,8,128]{3,2,1,0:T(8,128)(2,1)S(1)} %get-tuple-element.41.own_ref), channel_id=1, source_target_pairs={{0,8},{8,0},{16,24},{24,16},{32,40},{40,32},{48,56},{56,48},{64,72... | collective-permute-start | bytes 24584 | tf_op jit(solution)/shard_map/ppermute | solution.py:294
  32.5 6.1 %collective-permute-start.5 = (bf16[12,8,128]{2,1,0:T(8,128)(2,1)S(1)}, bf16[12,8,128]{2,1,0:T(8,128)(2,1)S(1)}, u32[]{:S(2)}, u32[]{:S(2)}) collective-permute-start(bf16[12,8,128]{2,1,0:T(8,128)(2,1)S(1)} %get-tuple-element.47), channel_id=1, source_target_pairs={{0,1},{1,2},{2,3},{3,4},{4,5},{5,6},{6,7},{7,0},{8,15},{9,8},{10,9... | collective-permute-start | bytes 73736 | tf_op jit(solution)/shard_map/ppermute | solution.py:308
  35.8 2.9 %collective-permute-start.4 = (bf16[4,2,8,128]{3,2,1,0:T(8,128)(2,1)S(1)}, bf16[4,2,8,128]{3,2,1,0:T(8,128)(2,1)S(1)}, u32[]{:S(2)}, u32[]{:S(2)}) collective-permute-start(bf16[4,2,8,128]{3,2,1,0:T(8,128)(2,1)S(1)} %get-tuple-element.46), channel_id=1, source_target_pairs={{0,16},{8,120},{16,32},{24,8},{32,48},{40,24},{48,64},{56,40},{64,... | collective-permute-start | bytes 49160 | tf_op jit(solution)/shard_map/ppermute | solution.py:313
  38.7 2.4 %collective-permute-start.6 = (bf16[2,3,8,128]{3,2,1,0:T(8,128)(2,1)S(1)}, bf16[2,3,8,128]{3,2,1,0:T(8,128)(2,1)S(1)}, u32[]{:S(2)}, u32[]{:S(2)}) collective-permute-start(bf16[2,3,8,128]{3,2,1,0:T(8,128)(2,1)S(1)} %get-tuple-element.52), channel_id=1, source_target_pairs={{0,8},{8,0},{16,24},{24,16},{32,40},{40,32},{48,56},{56,48},{64,72... | collective-permute-start | bytes 36872 | tf_op jit(solution)/shard_map/ppermute | solution.py:294
